TPU v7x, 256 devices: a whole 4x4x8 slice. The times are simulated.
256 devices in a mesh: blk: 16 (over y_lo, z), panel: 16 (over x, y_hi, core).
Axes of the slice: x: 4, y: 4 (y_hi: 2, y_lo: 2; y = y_hi * 2 + y_lo), z: 8, core: 2. Of those that a mesh axis runs over, the one named last changes fastest.
Arguments:
- left_env: bfloat16 [16, 320, 16128], P('blk', 'panel'), may hold values from -6 to 6
- right_env: bfloat16 [16, 320, 16128], P('blk', 'panel'), may hold values from -6 to 6
- site_tensors: bfloat16 [16, 320, 2304], P('blk', 'panel'), may hold values from -0.625 to 0.625
- chain_operator: bfloat16 [28, 28, 4, 4], replicated, may hold values from -0.5 to 0.5
- targets: int32 [16, 320], P('blk', 'panel'), may hold values from 0 to 319, as said below
- sector_dims: int32 [320], replicated, may hold values from 12 to 24
Outputs:
- left_out: bfloat16 [16, 320, 16128], P('blk', 'panel')
- right_out: bfloat16 [16, 320, 16128], P('blk', 'panel')
Inputs may be any that keep to these rules, and one draw needn't show every extreme that they name: `targets`: for each site, sector p * 20 + j has right sector ((p + c_j) mod 16) * 20 + pi_j, with offsets c_j and a permutation pi of 20 slots that depend on the site only; each row is a permutation of the 320 sectors; each offset is taken by at most 2 slots, and one offset by exactly 2.
All inputs are finite; a program needn't handle non-finite values.
Results may differ from a plain program's by a relative error of at most 0.0076.
Values may be sent and summed in bfloat16 or wider, within the bound.
No kernel may reach another device: no remote copies, remote signals or barrier semaphores. Data moves between devices by JAX's collectives and lax.ppermute only.
A program may use at most 64 MiB of HBM per device.

v0:
```python
import functools
import jax
import jax.numpy as jnp
from jax import lax
from jax.experimental import pallas as pl
from jax.experimental.pallas import tpu as pltpu
from jax.sharding import PartitionSpec as P

WD, PHYS, BLK = 28, 4, 24
WPAD = 32
SEC = 20
GRP = 5
LANES = 128
TILES = 144
ENV = WD * BLK * BLK
F32, BF16 = jnp.float32, jnp.bfloat16


def lane_ids(rows):
    return lax.broadcasted_iota(jnp.int32, (rows, LANES), 1)


def between(lane, low, high):
    return (lane >= low) & (lane < high)


def flat_to_rows(tiles, group, steps, rows):
    lane = lane_ids(steps)
    for b in range(16):
        acc = jnp.zeros((steps, LANES), F32)
        for c in range(GRP):
            first, last = 24 * b // LANES, (24 * b + 23) // LANES
            cut = 24 * c + (LANES * last - 24 * b if last > first else 24)
            for r in range(first, last + 1):
                piece = tiles[pl.ds((group * GRP + c) * 3 * steps + r, steps, stride=3), :]
                shift = (24 * c - 24 * b) % LANES
                if shift:
                    piece = pltpu.roll(piece, shift, 1)
                low, high = (24 * c, cut) if r == first else (cut, 24 * c + 24)
                acc = jnp.where(between(lane, low, high), piece, acc)
        rows[pl.ds(b, steps, stride=16), :] = acc


def rows_to_flat(rows, group, steps, tiles):
    lane = lane_ids(steps)
    for c in range(GRP):
        for r in range(3):
            acc = jnp.zeros((steps, LANES), F32)
            for b in range(16):
                low, high = max(24 * b - LANES * r, 0), min(24 * b + 24 - LANES * r, LANES)
                if low >= high:
                    continue
                piece = rows[pl.ds(b, steps, stride=16), :]
                shift = (24 * b - 24 * c) % LANES
                if shift:
                    piece = pltpu.roll(piece, shift, 1)
                acc = jnp.where(between(lane, low, high), piece, acc)
            tiles[pl.ds((group * GRP + c) * 3 * steps + r, steps, stride=3), :] = acc


def load_raw(raw, tiles, count):
    pad = tiles.shape[0] // SEC
    for n in range(count):
        tiles[pl.ds(n, SEC, stride=pad), :] = raw[:, n * LANES:(n + 1) * LANES].astype(F32)


def store_raw(tiles, raw, count):
    pad = tiles.shape[0] // SEC
    for n in range(count):
        raw[:, n * LANES:(n + 1) * LANES] = tiles[pl.ds(n, SEC, stride=pad), :].astype(BF16)


def load_wire(wire, tiles):
    for q in range(16):
        for m in range(SEC // 2):
            pair = wire[q, 16 * m:16 * m + 16, :].astype(F32)
            at = 2 * m * TILES + 8 * q
            tiles[at:at + 8, :] = pair[:8]
            tiles[at + TILES:at + TILES + 8, :] = pair[8:]


def store_wire(tiles, wire):
    for q in range(16):
        for m in range(SEC // 2):
            at = 2 * m * TILES + 8 * q
            pair = jnp.concatenate([tiles[at:at + 8, :], tiles[at + TILES:at + TILES + 8, :]], 0)
            wire[q, 16 * m:16 * m + 16, :] = pair.astype(BF16)


def site_rows(blocks, group, rows, spread):
    flat_to_rows(blocks, group, 8, rows)
    for s in range(PHYS):
        spread[pl.ds(s, BLK, stride=PHYS), :] = rows[s * BLK:(s + 1) * BLK, :]


def diagonal(rows, s):
    lane = lane_ids(BLK)
    block = rows[s * BLK:(s + 1) * BLK, :]
    parts = [jnp.where(between(lane, 24 * c, 24 * c + 24), block, 0.0) for c in range(GRP)]
    parts.append(jnp.zeros((8, LANES), F32))
    return jnp.concatenate(parts, 0)


def left_step(rows, rows_a, spread_a, operator, middle):
    diag = jnp.concatenate([diagonal(rows_a, s) for s in range(PHYS)], 1).astype(BF16)
    last = spread_a[...].T.astype(BF16)
    for p in range(6):
        env = jnp.concatenate([rows[pl.ds(4 * p + d, WPAD, stride=BLK), :] for d in range(4)], 0).astype(BF16)
        x = jnp.dot(env, diag, preferred_element_type=F32).astype(BF16)
        x = jnp.concatenate(
            [jnp.concatenate([x[:64, s * LANES:(s + 1) * LANES], x[64:, s * LANES:(s + 1) * LANES]], 1) for s in range(PHYS)], 0)
        y = jnp.dot(operator[...], x, preferred_element_type=F32)
        even = y[:, :LANES].reshape(WD, 8, LANES)
        odd = y[:, LANES:].reshape(WD, 8, LANES)
        middle[:, 16 * p:16 * p + 16, :] = jnp.concatenate([even, odd], 1).astype(BF16)
    lane = lane_ids(BLK)
    for u in range(WD // 2):
        y = jnp.concatenate([middle[2 * u], middle[2 * u + 1]], 1)
        out = jnp.dot(last, y, preferred_element_type=F32)
        for h in range(2):
            half = out[:, h * LANES:(h + 1) * LANES]
            acc = jnp.zeros((BLK, LANES), F32)
            for c in range(GRP):
                acc = jnp.where(between(lane, 24 * c, 24 * c + 24), half[24 * c:24 * c + 24], acc)
            rows[(2 * u + h) * BLK:(2 * u + h + 1) * BLK, :] = acc


def right_step(rows, rows_a, spread_a, operator, middle):
    first = spread_a[...].astype(BF16)
    diag = jnp.concatenate([diagonal(rows_a, s).T for s in range(PHYS)], 0).astype(BF16)
    lane = lane_ids(BLK)
    zeros = jnp.zeros((8, LANES), F32)
    for u in range(WD // 2):
        halves = []
        for h in range(2):
            block = rows[(2 * u + h) * BLK:(2 * u + h + 1) * BLK, :]
            parts = [jnp.where(between(lane, 24 * c, 24 * c + 24), block, 0.0) for c in range(GRP)]
            halves.append(jnp.concatenate(parts + [zeros], 0))
        z = jnp.dot(first, jnp.concatenate(halves, 1).astype(BF16), preferred_element_type=F32)
        even = z[:, :LANES].reshape(12, 8, LANES)
        odd = z[:, LANES:].reshape(12, 8, LANES)
        middle[:, 16 * u:16 * u + 16, :] = jnp.concatenate([even, odd], 1).astype(BF16)
    for p in range(6):
        z = jnp.concatenate([middle[2 * p], middle[2 * p + 1]], 1)
        v = jnp.dot(operator[...], z, preferred_element_type=F32).astype(BF16)
        v = jnp.concatenate(
            [jnp.concatenate([v[64 * t:64 * t + 64, h * LANES:(h + 1) * LANES] for t in range(PHYS)], 1) for h in range(2)], 0)
        out = jnp.dot(v, diag, preferred_element_type=F32)
        for d in range(4):
            rows[pl.ds(4 * p + d, WPAD, stride=BLK), :] = out[d * WPAD:(d + 1) * WPAD, :]


def env_kernel(steps, source, result, *refs):
    env, refs = refs[0], refs[1:]
    sites, refs = refs[:len(steps)], refs[len(steps):]
    operator, out, tiles, rows, rows_a, spread_a, middle = refs[:7]
    blocks = refs[7:]
    for c in range(SEC):
        tiles[c * TILES + 120:(c + 1) * TILES, :] = jnp.zeros((TILES - 120, LANES), F32)
    if source == "raw":
        load_raw(env, tiles, ENV // LANES)
    else:
        load_wire(env, tiles)
    for site, block in zip(sites, blocks):
        for c in range(SEC):
            block[c * 24 + 16:c * 24 + 24, :] = jnp.zeros((8, LANES), F32)
        load_raw(site, block, 18)

    def one(group, carry):
        flat_to_rows(tiles, group, 48, rows)
        for step, block in zip(steps, blocks):
            site_rows(block, group, rows_a, spread_a)
            (left_step if step == "L" else right_step)(rows, rows_a, spread_a, operator, middle)
        rows_to_flat(rows, group, 48, tiles)
        return carry

    lax.fori_loop(0, SEC // GRP, one, 0)
    if result == "raw":
        store_raw(tiles, out, ENV // LANES)
    else:
        store_wire(tiles, out)


def update(steps, source, result, env, sites, operator):
    shape = (SEC, ENV) if result == "raw" else (16, 160, LANES)
    middle = (WD, 96, LANES) if steps[0] == "L" else (12, 224, LANES)
    return pl.pallas_call(
        functools.partial(env_kernel, steps, source, result),
        out_shape=jax.ShapeDtypeStruct(shape, BF16),
        in_specs=[pl.BlockSpec(memory_space=pltpu.VMEM)] * (2 + len(sites)),
        out_specs=pl.BlockSpec(memory_space=pltpu.VMEM),
        scratch_shapes=[
            pltpu.VMEM((SEC * TILES, LANES), F32),
            pltpu.VMEM((WPAD * BLK, LANES), F32),
            pltpu.VMEM((LANES, LANES), F32),
            pltpu.VMEM((PHYS * BLK, LANES), F32),
            pltpu.VMEM(middle, BF16),
        ] + [pltpu.VMEM((SEC * 24, LANES), F32)] * len(sites),
        compiler_params=pltpu.CompilerParams(vmem_limit_bytes=40 * 1024 * 1024),
        cost_estimate=pl.CostEstimate(flops=2000000000 * len(sites), bytes_accessed=2000000, transcendentals=0),
        name="update_" + "".join(steps).lower(),
    )(env, *sites, operator)


def left_operator(op):
    same = jnp.eye(2, dtype=BF16)
    wide = jnp.pad(op, ((0, WPAD - WD), (0, 0), (0, 0), (0, 0)))
    return jnp.einsum("wvts,ab->vatsbw", wide, same).reshape(WD * 8, 8 * WPAD)


def right_operator(op):
    same = jnp.eye(2, dtype=BF16)
    wide = jnp.pad(op, ((0, WPAD - WD), (0, 0), (0, 0), (0, 0)))
    return jnp.einsum("wvts,ab->tawvbs", wide, same).reshape(8 * WPAD, WD * 8)


def permute_kernel(order, wire, out, held):
    for q in range(16):
        for m in range(SEC // 2):
            at = (q * SEC + 2 * m) * 8
            held[at:at + 16, :] = wire[q, 16 * m:16 * m + 16, :].astype(F32)
    for q in range(16):
        for m in range(SEC // 2):
            pair = [held[pl.ds(pl.multiple_of(order[q * SEC + 2 * m + h] * 8, 8), 8), :] for h in range(2)]
            out[q, 16 * m:16 * m + 16, :] = jnp.concatenate(pair, 0).astype(BF16)


def permute(order, wire):
    return pl.pallas_call(
        permute_kernel,
        out_shape=jax.ShapeDtypeStruct(wire.shape, BF16),
        in_specs=[pl.BlockSpec(memory_space=pltpu.SMEM), pl.BlockSpec(memory_space=pltpu.VMEM)],
        out_specs=pl.BlockSpec(memory_space=pltpu.VMEM),
        scratch_shapes=[pltpu.VMEM((16 * 160, LANES), F32)],
        compiler_params=pltpu.CompilerParams(vmem_limit_bytes=16 * 1024 * 1024),
        cost_estimate=pl.CostEstimate(flops=1000000, bytes_accessed=1400000, transcendentals=0),
        name="permute",
    )(order, wire)


def shifted(x, by):
    length = lax.axis_size("blk")
    return lax.ppermute(x, "blk", [(i, (i + by) % length) for i in range(length)])


def exchanged(x):
    return lax.all_to_all(x, "panel", split_axis=0, concat_axis=0, tiled=True)


def spread_and_collect(wire, order):
    return exchanged(permute(order, exchanged(wire)))


def pick(values, index):
    hits = index[:, None] == jnp.arange(values.shape[0])[None, :]
    return jnp.sum(jnp.where(hits, values[None, :], 0), axis=1)


def right_order(c0, s0, c1, s1):
    panels = jnp.arange(16)[:, None]
    offset, slot = c1 + pick(c0, s1), pick(s0, s1)
    return ((panels + offset[None, :]) % 16 * SEC + slot[None, :]).reshape(-1)


def left_order(c1, s1, c2, s2):
    panels = jnp.arange(16)[:, None]
    offset, slot = c2 + pick(c1, s2), pick(s1, s2)
    hits = jnp.arange(SEC)[:, None] == slot[None, :]
    source = jnp.sum(jnp.where(hits, jnp.arange(SEC)[None, :], 0), axis=1)
    back = jnp.sum(jnp.where(hits, offset[None, :], 0), axis=1)
    return ((panels - back[None, :]) % 16 * SEC + source[None, :]).reshape(-1)


def fetch_sites(blocks, me, c1, s1):
    slots = jnp.arange(SEC)
    rank = jnp.sum((c1[None, :] == c1[:, None]) & (slots[None, :] < slots[:, None]), axis=1)
    place = jnp.arange(32)
    wanted = ((me - place // 2) % 16)[:, None] == c1[None, :]
    wanted = wanted & ((place % 2)[:, None] == rank[None, :])
    send = jnp.sum(jnp.where(wanted[:, :, None] & (s1[:, None] == slots[None, :])[None], 1.0, 0.0), axis=1)
    packed = jnp.dot(send.astype(BF16), blocks, preferred_element_type=F32).astype(BF16)
    arrived = exchanged(packed.reshape(16, 2, -1)).reshape(32, -1)
    take = ((me + c1) % 16 * 2 + rank)[:, None] == place[None, :]
    return jnp.dot(take.astype(BF16), arrived, preferred_element_type=F32).astype(BF16)


def masked(tensor, rows, cols):
    place = jnp.arange(tensor.shape[1])
    keep = ((place // BLK % BLK)[None, :] < rows[:, None]) & ((place % BLK)[None, :] < cols[:, None])
    return jnp.where(keep, tensor, jnp.zeros((), BF16))


def body(left_env, right_env, site_tensors, chain_operator, targets, sector_dims):
    me = lax.axis_index("panel")
    target = targets[0]
    rows = lax.dynamic_slice_in_dim(sector_dims, me * SEC, SEC)
    blocks = masked(site_tensors[0], rows, pick(sector_dims, target))
    code = (target // SEC - me) % 16 * SEC + target % SEC
    code1, code2 = shifted(code, 1), shifted(code, 2)
    c0, s0, c1, s1, c2, s2 = code // SEC, code % SEC, code1 // SEC, code1 % SEC, code2 // SEC, code2 % SEC
    blocks1 = shifted(blocks, 1)

    wire = jnp.pad(right_env[0], ((0, 0), (0, 256))).reshape(SEC, 16, 8, LANES)
    wire = wire.transpose(1, 0, 2, 3).reshape(16, 160, LANES)
    arrived = spread_and_collect(wire, right_order(c0, s0, c1, s1))
    fetched = fetch_sites(blocks, me, c1, s1)
    right = update(("R", "R"), "wire", "raw", arrived, [fetched, blocks1], right_operator(chain_operator))
    right_out = shifted(right, -2)

    operator = left_operator(chain_operator)
    left = update(("L",), "raw", "wire", left_env[0], [blocks], operator)
    left = shifted(left, 2)
    left = update(("L",), "wire", "wire", left, [shifted(fetched, 1)], operator)
    left = spread_and_collect(left, left_order(c1, s1, c2, s2))
    left_out = left.reshape(16, SEC, 8, LANES).transpose(1, 0, 2, 3).reshape(SEC, -1)[:, :ENV]
    return left_out[None], right_out[None]


def solution(mesh):
    whole = P("blk", "panel", None)
    return jax.shard_map(
        body,
        mesh=mesh,
        in_specs=(whole, whole, whole, P(), P("blk", "panel"), P()),
        out_specs=(whole, whole),
        check_vma=False,
    )
```

profile of v0, /device:TPU:1, one launch (start us, length us, event | category | flops | bytes accessed | tf_op | source)
XLA Modules:
  0.0 146.1 jit_solution(14345693422391805265)
XLA Ops:
  0.6 0.6 copy-done.4
  1.3 2.5 %collective-permute-start.1 = (s32[20]{0:T(128)S(1)}, s32[20]{0:T(128)S(1)}, u32[]{:S(2)}, u32[]{:S(2)}) collective-permute-start(s32[20]{0:T(128)S(1)} %fusion.17), channel_id=1, source_target_pairs={{0,16},{16,32},{32,48},{48,64},{64,80},{80,96},{96,112},{112,128},... | collective-permute-start | bytes 248 | tf_op jit(solution)/shard_map/ppermute | solution.py:243
  3.9 3.0 %collective-permute-start = (s32[20]{0:T(128)S(1)}, s32[20]{0:T(128)S(1)}, u32[]{:S(2)}, u32[]{:S(2)}) collective-permute-start(s32[20]{0:T(128)S(1)} %fusion.17), channel_id=1, source_target_pairs={{0,32},{16,48},{32,64},{48,80},{64,96},{80,112},{96,128},{112,144}... | collective-permute-start | bytes 248 | tf_op jit(solution)/shard_map/ppermute | solution.py:243
  6.9 0.7 copy-done.3
  7.8 1.0 and_select_fusion.refs_1_
  8.8 2.9 %collective-permute-start.4 = (bf16[20,2304]{1,0:T(8,128)(2,1)S(1)}, bf16[20,2304]{1,0:T(8,128)(2,1)S(1)}, u32[]{:S(2)}, u32[]{:S(2)}) collective-permute-start(bf16[20,2304]{1,0:T(8,128)(2,1)S(1)} %and_select_fusion.refs_1_), channel_id=1, source_target_pairs={{0,16},{16,32},{32,48},{48,64},{64,80},{80,96},{96,112},{112,128},... | collective-permute-start | bytes 276488 | tf_op jit(solution)/shard_map/ppermute | solution.py:243
  11.8 1.2 pad.10
  13.1 1.0 copy_bitcast_fusion
  14.1 8.6 %all-to-all-start.3 = ((bf16[16,160,128]{2,1,0:T(8,128)(2,1)}), bf16[16,160,128]{2,1,0:T(8,128)(2,1)S(1)}, u32[]{:S(2)}, u32[]{:S(2)}) async-start(bf16[16,160,128]{2,1,0:T(8,128)(2,1)} %copy_bitcast_fusion), calls=%async_computation.3 | async-start | bytes 1310720 | tf_op jit(solution)/shard_map/all_to_all | solution.py:247
  23.0 1.3 multiply_bitcast_fusion
  24.3 0.4 copy.18
  24.8 0.3 reshape.181.refs_2_
  25.1 0.4 copy-done
  25.4 10.6 %update_l.2 = bf16[16,160,128]{2,1,0:T(8,128)(2,1)S(1)} custom-call(bf16[20,16128]{1,0:T(8,128)(2,1)S(1)} %bitcast.42, bf16[20,2304]{1,0:T(8,128)(2,1)S(1)} %and_select_fusion.refs_1_, bf16[224,256]{1,0:T(8,128)(2,1)S(1)} %reshape.181.refs_2_), custom_call_target="tpu_custom_call" | custom-call | flops 2000000000 | bytes 2000000 | tf_op jit(solution)/shard_map/update_l/pallas_call | solution.py:187
  36.1 1.3 collective-permute-start.2
  37.4 0.3 reshape.188
  38.9 0.7 reshape.182
  39.6 7.5 %all-to-all-start = ((bf16[16,2,2304]{2,1,0:T(2,128)(2,1)}), bf16[16,2,2304]{2,1,0:T(2,128)(2,1)S(1)}, u32[]{:S(2)}, u32[]{:S(2)}) async-start(bf16[16,2,2304]{2,1,0:T(2,128)(2,1)} %reshape.182), calls=%async_computation | async-start | bytes 294912 | tf_op jit(solution)/shard_map/all_to_all | solution.py:247
  47.1 1.7 %permute.3 = bf16[16,160,128]{2,1,0:T(8,128)(2,1)} custom-call(s32[320]{0:T(512)S(1)} %fusion.16.order, bf16[16,160,128]{2,1,0:T(8,128)(2,1)S(1)} %all-to-all-done.3.wire), custom_call_target="tpu_custom_call" | custom-call | flops 1000000 | bytes 1400000 | tf_op jit(solution)/shard_map/permute/pallas_call | solution.py:229
  48.8 7.7 %all-to-all-done = bf16[16,2,2304]{2,1,0:T(2,128)(2,1)S(1)} async-done(((bf16[16,2,2304]{2,1,0:T(2,128)(2,1)}), bf16[16,2,2304]{2,1,0:T(2,128)(2,1)S(1)}, u32[]{:S(2)}, u32[]{:S(2)}) %all-to-all-start) | async-done | bytes 147488 | tf_op jit(solution)/shard_map/all_to_all | solution.py:247
  56.6 4.5 %all-to-all-start.4 = ((bf16[16,160,128]{2,1,0:T(8,128)(2,1)}), bf16[16,160,128]{2,1,0:T(8,128)(2,1)S(1)}, u32[]{:S(2)}, u32[]{:S(2)}) async-start(bf16[16,160,128]{2,1,0:T(8,128)(2,1)} %permute.3), calls=%async_computation.4 | async-start | bytes 1310720 | tf_op jit(solution)/shard_map/all_to_all | solution.py:247
  61.4 0.3 collective-permute-start.3
  61.8 13.2 %collective-permute-done.3.refs_1_ = bf16[20,2304]{1,0:T(8,128)(2,1)S(1)} collective-permute-done((bf16[20,2304]{1,0:T(8,128)(2,1)S(1)}, bf16[20,2304]{1,0:T(8,128)(2,1)S(1)}, u32[]{:S(2)}, u32[]{:S(2)}) %collective-permute-start.3) | collective-permute-done | bytes 92192 | tf_op jit(solution)/shard_map/ppermute | solution.py:243
  74.9 11.1 %update_l.3 = bf16[16,160,128]{2,1,0:T(8,128)(2,1)} custom-call(bf16[16,160,128]{2,1,0:T(8,128)(2,1)S(1)} %collective-permute-done.2.refs_0_, bf16[20,2304]{1,0:T(8,128)(2,1)S(1)} %collective-permute-done.3.refs_1_, bf16[224,256]{1,0:T(8,128)(2,1)S(1)} %reshape.181.refs_2_), custom_call_target="tpu_custom_call" | custom-call | flops 2000000000 | bytes 2000000 | tf_op jit(solution)/shard_map/update_l/pallas_call | solution.py:187
  86.0 6.9 %all-to-all-start.1 = ((bf16[16,160,128]{2,1,0:T(8,128)(2,1)}), bf16[16,160,128]{2,1,0:T(8,128)(2,1)S(1)}, u32[]{:S(2)}, u32[]{:S(2)}) async-start(bf16[16,160,128]{2,1,0:T(8,128)(2,1)} %update_l.3), calls=%async_computation.1 | async-start | bytes 1310720 | tf_op jit(solution)/shard_map/all_to_all | solution.py:247
  93.1 14.3 %update_rr.1 = bf16[20,16128]{1,0:T(8,128)(2,1)S(1)} custom-call(bf16[16,160,128]{2,1,0:T(8,128)(2,1)S(1)} %all-to-all-done.4.refs_0_, bf16[20,2304]{1,0:T(8,128)(2,1)S(1)} %convolution_convert_fusion.1.refs_1_, bf16[20,2304]{1,0:T(8,128)(2,1)S(1)} %collective-permute-done.4.refs_2_, bf16[256,224]{1,0:T(8,128)(2,1)S(1)} %copy.21.refs_3_), custom_call_target="tpu_custom_call" | custom-call | flops 4000000000 | bytes 2000000 | tf_op jit(solution)/shard_map/update_rr/pallas_call | solution.py:187
  107.5 1.7 %permute.2 = bf16[16,160,128]{2,1,0:T(8,128)(2,1)} custom-call(s32[320]{0:T(512)S(1)} %fusion.13.order, bf16[16,160,128]{2,1,0:T(8,128)(2,1)S(1)} %all-to-all-done.1.wire), custom_call_target="tpu_custom_call" | custom-call | flops 1000000 | bytes 1400000 | tf_op jit(solution)/shard_map/permute/pallas_call | solution.py:229
  109.2 7.2 %all-to-all-start.2 = ((bf16[16,160,128]{2,1,0:T(8,128)(2,1)}), bf16[16,160,128]{2,1,0:T(8,128)(2,1)S(1)}, u32[]{:S(2)}, u32[]{:S(2)}) async-start(bf16[16,160,128]{2,1,0:T(8,128)(2,1)} %permute.2), calls=%async_computation.2 | async-start | bytes 1310720 | tf_op jit(solution)/shard_map/all_to_all | solution.py:247
  116.5 27.1 %collective-permute-done.5 = bf16[20,16128]{1,0:T(8,128)(2,1)S(1)} collective-permute-done((bf16[20,16128]{1,0:T(8,128)(2,1)S(1)}, bf16[20,16128]{1,0:T(8,128)(2,1)S(1)}, u32[]{:S(2)}, u32[]{:S(2)}) %collective-permute-start.5) | collective-permute-done | bytes 645152 | tf_op jit(solution)/shard_map/ppermute | solution.py:243
  143.8 0.5 copy.23
  144.3 0.9 slice_bitcast_fusion
  145.2 0.9 copy.28
  (53 shorter events, 2.9 us)
Async XLA Ops:
  0.6 0.7 copy-start.4
  1.3 36.5 %collective-permute-start.1 = (s32[20]{0:T(128)S(1)}, s32[20]{0:T(128)S(1)}, u32[]{:S(2)}, u32[]{:S(2)}) collective-permute-start(s32[20]{0:T(128)S(1)} %fusion.17), channel_id=1, source_target_pairs={{0,16},{16,32},{32,48},{48,64},{64,80},{80,96},{96,112},{112,128},... | collective-permute-start | bytes 248 | tf_op jit(solution)/shard_map/ppermute | solution.py:243
  3.9 34.0 %collective-permute-start = (s32[20]{0:T(128)S(1)}, s32[20]{0:T(128)S(1)}, u32[]{:S(2)}, u32[]{:S(2)}) collective-permute-start(s32[20]{0:T(128)S(1)} %fusion.17), channel_id=1, source_target_pairs={{0,32},{16,48},{32,64},{48,80},{64,96},{80,112},{96,128},{112,144}... | collective-permute-start | bytes 248 | tf_op jit(solution)/shard_map/ppermute | solution.py:243
  6.9 0.7 copy-start.3
  8.8 84.3 %collective-permute-start.4 = (bf16[20,2304]{1,0:T(8,128)(2,1)S(1)}, bf16[20,2304]{1,0:T(8,128)(2,1)S(1)}, u32[]{:S(2)}, u32[]{:S(2)}) collective-permute-start(bf16[20,2304]{1,0:T(8,128)(2,1)S(1)} %and_select_fusion.refs_1_), channel_id=1, source_target_pairs={{0,16},{16,32},{32,48},{48,64},{64,80},{80,96},{96,112},{112,128},... | collective-permute-start | bytes 276488 | tf_op jit(solution)/shard_map/ppermute | solution.py:243
  14.1 8.6 %copy-start.2 = (bf16[28,28,4,4]{1,3,2,0:T(4,128)(2,1)S(1)}, bf16[28,28,4,4]{1,3,2,0:T(4,128)(2,1)}, u32[]{:S(2)}) copy-start(bf16[28,28,4,4]{1,3,2,0:T(4,128)(2,1)} %param.9) | copy-start | bytes 75268
  14.1 25.5 %all-to-all-start.3 = ((bf16[16,160,128]{2,1,0:T(8,128)(2,1)}), bf16[16,160,128]{2,1,0:T(8,128)(2,1)S(1)}, u32[]{:S(2)}, u32[]{:S(2)}) async-start(bf16[16,160,128]{2,1,0:T(8,128)(2,1)} %copy_bitcast_fusion), calls=%async_computation.3 | async-start | bytes 1310720 | tf_op jit(solution)/shard_map/all_to_all | solution.py:247
  24.3 1.1 copy-start
  25.4 12.0 %copy-start.1 = (bf16[4,2,32,28,2,4]{2,1,0,5,4,3:T(2,128)(2,1)S(1)}, bf16[4,2,32,28,2,4]{2,1,0,5,4,3:T(2,128)(2,1)}, u32[]{:S(2)}) copy-start(bf16[4,2,32,28,2,4]{2,1,0,5,4,3:T(2,128)(2,1)} %get-tuple-element.11) | copy-start | bytes 344068
  36.1 38.9 %collective-permute-start.2 = (bf16[16,160,128]{2,1,0:T(8,128)(2,1)S(1)}, bf16[16,160,128]{2,1,0:T(8,128)(2,1)S(1)}, u32[]{:S(2)}, u32[]{:S(2)}) collective-permute-start(bf16[16,160,128]{2,1,0:T(8,128)(2,1)S(1)} %update_l.2), channel_id=1, source_target_pairs={{0,32},{16,48},{32,64},{48,80},{64,96},{80,112},{96,128},{112,144}... | collective-permute-start | bytes 1966088 | tf_op jit(solution)/shard_map/ppermute | solution.py:243
  39.6 16.9 %all-to-all-start = ((bf16[16,2,2304]{2,1,0:T(2,128)(2,1)}), bf16[16,2,2304]{2,1,0:T(2,128)(2,1)S(1)}, u32[]{:S(2)}, u32[]{:S(2)}) async-start(bf16[16,2,2304]{2,1,0:T(2,128)(2,1)} %reshape.182), calls=%async_computation | async-start | bytes 294912 | tf_op jit(solution)/shard_map/all_to_all | solution.py:247
  56.6 29.4 %all-to-all-start.4 = ((bf16[16,160,128]{2,1,0:T(8,128)(2,1)}), bf16[16,160,128]{2,1,0:T(8,128)(2,1)S(1)}, u32[]{:S(2)}, u32[]{:S(2)}) async-start(bf16[16,160,128]{2,1,0:T(8,128)(2,1)} %permute.3), calls=%async_computation.4 | async-start | bytes 1310720 | tf_op jit(solution)/shard_map/all_to_all | solution.py:247
  61.4 13.5 %collective-permute-start.3 = (bf16[20,2304]{1,0:T(8,128)(2,1)S(1)}, bf16[20,2304]{1,0:T(8,128)(2,1)S(1)}, u32[]{:S(2)}, u32[]{:S(2)}) collective-permute-start(bf16[20,2304]{1,0:T(8,128)(2,1)S(1)} %convolution_convert_fusion.1.refs_1_), channel_id=1, source_target_pairs={{0,16},{16,32},{32,48},{48,64},{64,80},{80,96},{96,112},{112,128},... | collective-permute-start | bytes 276488 | tf_op jit(solution)/shard_map/ppermute | solution.py:243
  86.0 21.5 %all-to-all-start.1 = ((bf16[16,160,128]{2,1,0:T(8,128)(2,1)}), bf16[16,160,128]{2,1,0:T(8,128)(2,1)S(1)}, u32[]{:S(2)}, u32[]{:S(2)}) async-start(bf16[16,160,128]{2,1,0:T(8,128)(2,1)} %update_l.3), calls=%async_computation.1 | async-start | bytes 1310720 | tf_op jit(solution)/shard_map/all_to_all | solution.py:247
  107.4 36.1 %collective-permute-start.5 = (bf16[20,16128]{1,0:T(8,128)(2,1)S(1)}, bf16[20,16128]{1,0:T(8,128)(2,1)S(1)}, u32[]{:S(2)}, u32[]{:S(2)}) collective-permute-start(bf16[20,16128]{1,0:T(8,128)(2,1)S(1)} %update_rr.1), channel_id=1, source_target_pairs={{0,224},{16,240},{32,0},{48,16},{64,32},{80,48},{96,64},{112,80},{... | collective-permute-start | bytes 1935368 | tf_op jit(solution)/shard_map/ppermute | solution.py:243
  109.2 34.3 %all-to-all-start.2 = ((bf16[16,160,128]{2,1,0:T(8,128)(2,1)}), bf16[16,160,128]{2,1,0:T(8,128)(2,1)S(1)}, u32[]{:S(2)}, u32[]{:S(2)}) async-start(bf16[16,160,128]{2,1,0:T(8,128)(2,1)} %permute.2), calls=%async_computation.2 | async-start | bytes 1310720 | tf_op jit(solution)/shard_map/all_to_all | solution.py:247
where the time goes:
time: 147 us; the launch traced here: 146 us
  waiting for transfers between devices  48 us (33%)
  starting transfers between devices  44.8 us (30%)
  Pallas kernels  39.4 us (27%)
  local copies, waits for them, and re-layouts  9.21 us (6%)
  other arithmetic  3.35 us (2%)
    ppermute x6, waiting for transfers between devices, shifted(): lax.ppermute(x, 'blk', [(i, (i + by) % length) for i in range(length)])  40.2 us
    pallas_call x3, Pallas kernels, update(): pl.pallas_call(functools.partial(env_kernel, steps, source, result), out_...  35.9 us
    all_to_all x5, starting transfers between devices, exchanged(): return lax.all_to_all(x, 'panel', split_axis=0, concat_axis=0, tiled=True)  34.7 us
    ppermute x6, starting transfers between devices, shifted(): lax.ppermute(x, 'blk', [(i, (i + by) % length) for i in range(length)])  10.1 us
    all_to_all x5, waiting for transfers between devices, exchanged(): return lax.all_to_all(x, 'panel', split_axis=0, concat_axis=0, tiled=True)  7.73 us
    unnamed x16, local copies, waits for them, and re-layouts  3.74 us
    pallas_call x2, Pallas kernels, permute(): pl.pallas_call(permute_kernel, out_shape=jax.ShapeDtypeStruct(wire.shape,...  3.46 us
  transfers between devices with their start and end apart: 11, of which 3 were waited for; matrix products, arithmetic and copies ran while one was open for 6% of the time, Pallas kernels for 27%

commit v1 on v0

--- a/solution.py
+++ b/solution.py
@@ -9,6 +9,7 @@
 WD, PHYS, BLK = 28, 4, 24
 WPAD = 32
 SEC = 20
+FIRST, SECOND, WHOLE = (0, 2), (2, 2), (0, 4)
 GRP = 5
 LANES = 128
 TILES = 144
@@ -24,38 +25,58 @@
     return (lane >= low) & (lane < high)
 
 
+def spans(b):
+    out = []
+    for r in range(3):
+        low, high = max(24 * b - LANES * r, 0), min(24 * b + 24 - LANES * r, LANES)
+        if low < high:
+            out.append((r, low, high))
+    return out
+
+
+def merge(lane, pieces):
+    acc = None
+    for value, low, high in pieces:
+        acc = value if acc is None else jnp.where(between(lane, low, high), value, acc)
+    return acc
+
+
+def turned(value, shift):
+    return pltpu.roll(value, shift % LANES, 1) if shift % LANES else value
+
+
 def flat_to_rows(tiles, group, steps, rows):
     lane = lane_ids(steps)
+    live = lane < GRP * BLK
+    shifted_by = {}
+
+    def source(c, r):
+        return tiles[pl.ds((group * GRP + c) * 3 * steps + r, steps, stride=3), :]
+
     for b in range(16):
-        acc = jnp.zeros((steps, LANES), F32)
-        for c in range(GRP):
-            first, last = 24 * b // LANES, (24 * b + 23) // LANES
-            cut = 24 * c + (LANES * last - 24 * b if last > first else 24)
-            for r in range(first, last + 1):
-                piece = tiles[pl.ds((group * GRP + c) * 3 * steps + r, steps, stride=3), :]
-                shift = (24 * c - 24 * b) % LANES
-                if shift:
-                    piece = pltpu.roll(piece, shift, 1)
-                low, high = (24 * c, cut) if r == first else (cut, 24 * c + 24)
-                acc = jnp.where(between(lane, low, high), piece, acc)
-        rows[pl.ds(b, steps, stride=16), :] = acc
+        for d in range(-b, GRP - b):
+            if d not in shifted_by:
+                pieces = [(source(c, r), low, high) for c in range(GRP) if 0 <= c - d < 16 for r, low, high in spans(c - d)]
+                shifted_by[d] = turned(merge(lane, pieces), 24 * d)
+        acc = merge(lane, [(shifted_by[c - b], 24 * c, 24 * c + 24) for c in range(GRP)])
+        rows[pl.ds(b, steps, stride=16), :] = jnp.where(live, acc, 0.0)
+        del shifted_by[GRP - 1 - b]
 
 
 def rows_to_flat(rows, group, steps, tiles):
     lane = lane_ids(steps)
-    for c in range(GRP):
-        for r in range(3):
-            acc = jnp.zeros((steps, LANES), F32)
-            for b in range(16):
-                low, high = max(24 * b - LANES * r, 0), min(24 * b + 24 - LANES * r, LANES)
-                if low >= high:
-                    continue
-                piece = rows[pl.ds(b, steps, stride=16), :]
-                shift = (24 * b - 24 * c) % LANES
-                if shift:
-                    piece = pltpu.roll(piece, shift, 1)
-                acc = jnp.where(between(lane, low, high), piece, acc)
-            tiles[pl.ds((group * GRP + c) * 3 * steps + r, steps, stride=3), :] = acc
+    for r in range(3):
+        shifted_by = {}
+        inside = [(b, low, high) for b in range(16) for tile, low, high in spans(b) if tile == r]
+        for c in range(GRP):
+            pieces = []
+            for b, low, high in inside:
+                d = c - b
+                if d not in shifted_by:
+                    parts = [(rows[pl.ds(e - d, steps, stride=16), :], 24 * e, 24 * e + 24) for e in range(GRP) if 0 <= e - d < 16]
+                    shifted_by[d] = turned(merge(lane, parts), -24 * d)
+                pieces.append((shifted_by[d], low, high))
+            tiles[pl.ds((group * GRP + c) * 3 * steps + r, steps, stride=3), :] = merge(lane, pieces)
 
 
 def load_raw(raw, tiles, count):
@@ -150,44 +171,77 @@
             rows[pl.ds(4 * p + d, WPAD, stride=BLK), :] = out[d * WPAD:(d + 1) * WPAD, :]
 
 
-def env_kernel(steps, source, result, *refs):
-    env, refs = refs[0], refs[1:]
-    sites, refs = refs[:len(steps)], refs[len(steps):]
-    operator, out, tiles, rows, rows_a, spread_a, middle = refs[:7]
-    blocks = refs[7:]
-    for c in range(SEC):
-        tiles[c * TILES + 120:(c + 1) * TILES, :] = jnp.zeros((TILES - 120, LANES), F32)
-    if source == "raw":
-        load_raw(env, tiles, ENV // LANES)
-    else:
-        load_wire(env, tiles)
-    for site, block in zip(sites, blocks):
+def load_sites(site, block):
+    if site.shape[0] == SEC:
         for c in range(SEC):
             block[c * 24 + 16:c * 24 + 24, :] = jnp.zeros((8, LANES), F32)
         load_raw(site, block, 18)
-
-    def one(group, carry):
-        flat_to_rows(tiles, group, 48, rows)
+    else:
+        block[...] = site[...].astype(F32)
+
+
+def clear_tails(tiles):
+    for c in range(SEC):
+        tiles[c * TILES + 120:(c + 1) * TILES, :] = jnp.zeros((TILES - 120, LANES), F32)
+
+
+def load_part(part, tiles, groups):
+    for m in range(GRP * groups[1]):
+        at = (GRP * groups[0] + m) * TILES
+        tiles[at:at + LANES, :] = part[m].astype(F32)
+
+
+def store_part(tiles, part, groups):
+    for m in range(GRP * groups[1]):
+        at = (GRP * groups[0] + m) * TILES
+        part[m] = tiles[at:at + LANES, :].astype(BF16)
+
+
+def update_kernel(steps, source, result, groups, count, *refs):
+    env, sites, operator = refs[0], refs[1:1 + len(steps)], refs[1 + len(steps)]
+    refs = refs[count:]
+    out, tiles, rows, rows_a, spread_a, middle = refs[:6]
+    blocks = refs[6:]
+    if source != "rows":
+        clear_tails(tiles)
+        (load_raw if source == "raw" else load_wire)(env, tiles, *([ENV // LANES] if source == "raw" else []))
+    else:
+        rows[WD * BLK:, :] = jnp.zeros(((WPAD - WD) * BLK, LANES), F32)
+    for site, block in zip(sites, blocks):
+        load_sites(site, block)
+
+    def one(local, carry):
+        group = local + groups[0]
+        if source == "rows":
+            rows[:WD * BLK, :] = env[local].astype(F32)
+        else:
+            flat_to_rows(tiles, group, 48, rows)
         for step, block in zip(steps, blocks):
             site_rows(block, group, rows_a, spread_a)
             (left_step if step == "L" else right_step)(rows, rows_a, spread_a, operator, middle)
-        rows_to_flat(rows, group, 48, tiles)
+        if result == "rows":
+            out[local] = rows[:WD * BLK, :].astype(BF16)
+        else:
+            rows_to_flat(rows, group, 48, tiles)
         return carry
 
-    lax.fori_loop(0, SEC // GRP, one, 0)
-    if result == "raw":
+    lax.fori_loop(0, groups[1], one, 0)
+    if result == "part":
+        store_part(tiles, out, groups)
+    elif result == "raw":
         store_raw(tiles, out, ENV // LANES)
-    else:
+    elif result == "wire":
         store_wire(tiles, out)
 
 
-def update(steps, source, result, env, sites, operator):
-    shape = (SEC, ENV) if result == "raw" else (16, 160, LANES)
+def update(steps, source, result, groups, env, sites, operator, *tickets):
+    shape = {"rows": (groups[1], WD * BLK, LANES), "part": (GRP * groups[1], LANES, LANES), "wire": (16, 160, LANES), "raw": (SEC, ENV)}[result]
     middle = (WD, 96, LANES) if steps[0] == "L" else (12, 224, LANES)
+    inputs = [env, *sites, operator, *tickets]
     return pl.pallas_call(
-        functools.partial(env_kernel, steps, source, result),
+        functools.partial(update_kernel, steps, source, result, groups, len(inputs)),
         out_shape=jax.ShapeDtypeStruct(shape, BF16),
-        in_specs=[pl.BlockSpec(memory_space=pltpu.VMEM)] * (2 + len(sites)),
+        in_specs=[pl.BlockSpec(memory_space=pltpu.VMEM)] * (2 + len(sites)) + [pl.BlockSpec(memory_space=pl.ANY)] * len(tickets),
         out_specs=pl.BlockSpec(memory_space=pltpu.VMEM),
         scratch_shapes=[
             pltpu.VMEM((SEC * TILES, LANES), F32),
@@ -196,10 +250,10 @@
             pltpu.VMEM((PHYS * BLK, LANES), F32),
             pltpu.VMEM(middle, BF16),
         ] + [pltpu.VMEM((SEC * 24, LANES), F32)] * len(sites),
-        compiler_params=pltpu.CompilerParams(vmem_limit_bytes=40 * 1024 * 1024),
-        cost_estimate=pl.CostEstimate(flops=2000000000 * len(sites), bytes_accessed=2000000, transcendentals=0),
-        name="update_" + "".join(steps).lower(),
-    )(env, *sites, operator)
+        compiler_params=pltpu.CompilerParams(vmem_limit_bytes=32 * 1024 * 1024),
+        cost_estimate=pl.CostEstimate(flops=(2300000000 if steps[0] == "L" else 600000000) * groups[1] * len(sites), bytes_accessed=100000, transcendentals=0),
+        name="update_" + "".join(steps).lower() + str(groups[0]),
+    )(*inputs)
 
 
 def left_operator(op):
@@ -214,7 +268,31 @@
     return jnp.einsum("wvts,ab->tawvbs", wide, same).reshape(8 * WPAD, WD * 8)
 
 
-def permute_kernel(order, wire, out, held):
+def call(kernel, name, shapes, inputs, scratch, in_smem=0):
+    spaces = [pltpu.SMEM] * in_smem + [pltpu.VMEM] * (len(inputs) - in_smem)
+    return pl.pallas_call(
+        kernel,
+        out_shape=[jax.ShapeDtypeStruct(shape, BF16) for shape in shapes],
+        in_specs=[pl.BlockSpec(memory_space=space) for space in spaces],
+        out_specs=[pl.BlockSpec(memory_space=pltpu.VMEM)] * len(shapes),
+        scratch_shapes=scratch,
+        compiler_params=pltpu.CompilerParams(vmem_limit_bytes=32 * 1024 * 1024),
+        cost_estimate=pl.CostEstimate(flops=2000000000, bytes_accessed=100000, transcendentals=0),
+        name=name,
+    )(*inputs)
+
+
+def wire_kernel(raw, out, tiles):
+    clear_tails(tiles)
+    load_raw(raw, tiles, ENV // LANES)
+    store_wire(tiles, out)
+
+
+def to_wire(raw):
+    return call(wire_kernel, "to_wire", [(16, 160, LANES)], [raw], [pltpu.VMEM((SEC * TILES, LANES), F32)])[0]
+
+
+def permute_wire(order, wire, out, held):
     for q in range(16):
         for m in range(SEC // 2):
             at = (q * SEC + 2 * m) * 8
@@ -225,17 +303,61 @@
             out[q, 16 * m:16 * m + 16, :] = jnp.concatenate(pair, 0).astype(BF16)
 
 
+def permute_pack_kernel(order, chosen, wire, sites, sites1, out, held, block, block1):
+    permute_wire(order, wire, out, held)
+    load_sites(sites, block)
+    load_sites(sites1, block1)
+    for q in range(16):
+        for n, source in enumerate((block, block1)):
+            pair = [source[pl.ds(pl.multiple_of(chosen[32 * n + 2 * q + h] * 24, 8), 24), :] for h in range(2)]
+            out[q, 160 + 48 * n:208 + 48 * n, :] = jnp.concatenate(pair, 0).astype(BF16)
+
+
+def permute_pack(order, chosen, wire, sites, sites1):
+    scratch = [pltpu.VMEM((16 * 160, LANES), F32)] + [pltpu.VMEM((SEC * 24, LANES), F32)] * 2
+    return call(permute_pack_kernel, "permute_pack", [(16, 256, LANES)], [order, chosen, wire, sites, sites1], scratch, 2)[0]
+
+
+def fetch_kernel(places, wire, fetched, pushed, extra):
+    for q in range(16):
+        extra[q * 96:q * 96 + 96, :] = wire[q, 160:256, :].astype(F32)
+    for n, out in enumerate((fetched, pushed)):
+        for m in range(SEC // 2):
+            pair = [extra[pl.ds(pl.multiple_of(places[SEC * n + 2 * m + h] * 24, 8), 24), :] for h in range(2)]
+            out[48 * m:48 * m + 48, :] = jnp.concatenate(pair, 0).astype(BF16)
+
+
+def fetch(places, wire):
+    return call(fetch_kernel, "fetch", [(SEC * 24, LANES)] * 2, [places, wire], [pltpu.VMEM((16 * 96, LANES), F32)], 1)
+
+
+def touch_kernel(value, out):
+    out[...] = jnp.zeros((16, LANES), BF16)
+
+
+def touch(value):
+    return pl.pallas_call(
+        touch_kernel,
+        out_shape=jax.ShapeDtypeStruct((16, LANES), BF16),
+        in_specs=[pl.BlockSpec(memory_space=pl.ANY)],
+        out_specs=pl.BlockSpec(memory_space=pltpu.VMEM),
+        cost_estimate=pl.CostEstimate(flops=20000000000, bytes_accessed=1000, transcendentals=0),
+        name="touch",
+    )(value)
+
+
 def permute(order, wire):
-    return pl.pallas_call(
-        permute_kernel,
-        out_shape=jax.ShapeDtypeStruct(wire.shape, BF16),
-        in_specs=[pl.BlockSpec(memory_space=pltpu.SMEM), pl.BlockSpec(memory_space=pltpu.VMEM)],
-        out_specs=pl.BlockSpec(memory_space=pltpu.VMEM),
-        scratch_shapes=[pltpu.VMEM((16 * 160, LANES), F32)],
-        compiler_params=pltpu.CompilerParams(vmem_limit_bytes=16 * 1024 * 1024),
-        cost_estimate=pl.CostEstimate(flops=1000000, bytes_accessed=1400000, transcendentals=0),
-        name="permute",
-    )(order, wire)
+    return call(permute_wire, "permute", [(16, 160, LANES)], [order, wire], [pltpu.VMEM((16 * 160, LANES), F32)], 1)[0]
+
+
+def join_kernel(first, second, out, tiles):
+    load_part(first, tiles, FIRST)
+    load_part(second, tiles, SECOND)
+    store_raw(tiles, out, ENV // LANES)
+
+
+def join(first, second):
+    return call(join_kernel, "join", [(SEC, ENV)], [first, second], [pltpu.VMEM((SEC * TILES, LANES), F32)])[0]
 
 
 def shifted(x, by):
@@ -247,8 +369,8 @@
     return lax.all_to_all(x, "panel", split_axis=0, concat_axis=0, tiled=True)
 
 
-def spread_and_collect(wire, order):
-    return exchanged(permute(order, exchanged(wire)))
+def after(x, *others):
+    return lax.optimization_barrier((x, *others))[0]
 
 
 def pick(values, index):
@@ -271,17 +393,17 @@
     return ((panels - back[None, :]) % 16 * SEC + source[None, :]).reshape(-1)
 
 
-def fetch_sites(blocks, me, c1, s1):
+def move_plan(me, c1, s1):
     slots = jnp.arange(SEC)
     rank = jnp.sum((c1[None, :] == c1[:, None]) & (slots[None, :] < slots[:, None]), axis=1)
     place = jnp.arange(32)
-    wanted = ((me - place // 2) % 16)[:, None] == c1[None, :]
-    wanted = wanted & ((place % 2)[:, None] == rank[None, :])
-    send = jnp.sum(jnp.where(wanted[:, :, None] & (s1[:, None] == slots[None, :])[None], 1.0, 0.0), axis=1)
-    packed = jnp.dot(send.astype(BF16), blocks, preferred_element_type=F32).astype(BF16)
-    arrived = exchanged(packed.reshape(16, 2, -1)).reshape(32, -1)
-    take = ((me + c1) % 16 * 2 + rank)[:, None] == place[None, :]
-    return jnp.dot(take.astype(BF16), arrived, preferred_element_type=F32).astype(BF16)
+    same = (place % 2)[:, None] == rank[None, :]
+    asked = same & (((me - place // 2) % 16)[:, None] == c1[None, :])
+    pushed = same & (((place // 2 - me) % 16)[:, None] == c1[None, :])
+    chosen = [jnp.sum(jnp.where(asked, s1[None, :], 0), axis=1), jnp.sum(jnp.where(pushed, slots[None, :], 0), axis=1)]
+    landing = slots[:, None] == s1[None, :]
+    back = jnp.sum(jnp.where(landing, ((me - c1) % 16 * 4 + 2 + rank)[None, :], 0), axis=1)
+    return jnp.concatenate(chosen), jnp.concatenate([(me + c1) % 16 * 4 + rank, back])
 
 
 def masked(tensor, rows, cols):
@@ -292,27 +414,36 @@
 
 def body(left_env, right_env, site_tensors, chain_operator, targets, sector_dims):
     me = lax.axis_index("panel")
-    target = targets[0]
+    wire = to_wire(right_env[0])
+    arrived = exchanged(wire)
+
+    target = after(targets[0], wire)
+    code = (target // SEC - me) % 16 * SEC + target % SEC
     rows = lax.dynamic_slice_in_dim(sector_dims, me * SEC, SEC)
     blocks = masked(site_tensors[0], rows, pick(sector_dims, target))
-    code = (target // SEC - me) % 16 * SEC + target % SEC
-    code1, code2 = shifted(code, 1), shifted(code, 2)
-    c0, s0, c1, s1, c2, s2 = code // SEC, code % SEC, code1 // SEC, code1 % SEC, code2 // SEC, code2 % SEC
-    blocks1 = shifted(blocks, 1)
-
-    wire = jnp.pad(right_env[0], ((0, 0), (0, 256))).reshape(SEC, 16, 8, LANES)
-    wire = wire.transpose(1, 0, 2, 3).reshape(16, 160, LANES)
-    arrived = spread_and_collect(wire, right_order(c0, s0, c1, s1))
-    fetched = fetch_sites(blocks, me, c1, s1)
-    right = update(("R", "R"), "wire", "raw", arrived, [fetched, blocks1], right_operator(chain_operator))
-    right_out = shifted(right, -2)
-
-    operator = left_operator(chain_operator)
-    left = update(("L",), "raw", "wire", left_env[0], [blocks], operator)
-    left = shifted(left, 2)
-    left = update(("L",), "wire", "wire", left, [shifted(fetched, 1)], operator)
-    left = spread_and_collect(left, left_order(c1, s1, c2, s2))
-    left_out = left.reshape(16, SEC, 8, LANES).transpose(1, 0, 2, 3).reshape(SEC, -1)[:, :ENV]
+    operator = left_operator(after(chain_operator, wire))
+    left = update(("L",), "raw", "wire", WHOLE, left_env[0], [blocks], operator)
+    left_moved = shifted(left, 2)
+    code1, blocks1 = shifted(code, 1), shifted(blocks, 1)
+    code2 = shifted(after(code, left), 2)
+
+    c0, s0, c1, s1 = code // SEC, code % SEC, code1 // SEC, code1 % SEC
+    chosen, places = move_plan(me, c1, s1)
+    wire = permute_pack(right_order(c0, s0, c1, s1), chosen, after(arrived, left), blocks, blocks1)
+    right = exchanged(wire)
+    fetched, pushed = fetch(places, right)
+
+    operator_r = right_operator(after(chain_operator, wire))
+    left = exchanged(after(left_moved, fetched))
+    right0 = update(("R", "R"), "wire", "part", FIRST, right, [fetched, blocks1], operator_r, touch(left_moved))
+    right0_moved = shifted(right0, -2)
+    right1 = update(("R", "R"), "wire", "part", SECOND, after(right, right0), [fetched, blocks1], operator_r)
+    right1_moved = shifted(right1, -2)
+    code2 = after(code2, right0)
+    c2, s2 = code2 // SEC, code2 % SEC
+    left = exchanged(permute(left_order(c1, s1, c2, s2), after(left, right1)))
+    left_out = update(("L",), "wire", "raw", WHOLE, left, [pushed], operator, touch(right0_moved))
+    right_out = join(after(right0_moved, left_out), right1_moved)
     return left_out[None], right_out[None]
 
 

time: 147 us -> 120 us (0.82)
  the two profiles are of different devices: /device:TPU:1 before, /device:TPU:32 now
where the time goes in v1:
time: 120 us; the launch traced here: 119 us
  starting transfers between devices  39.6 us (33%)
  Pallas kernels  36.9 us (31%)
  waiting for transfers between devices  32.8 us (27%)
  local copies, waits for them, and re-layouts  6.43 us (5%)
  other arithmetic  2.29 us (2%)
    all_to_all x4, starting transfers between devices, exchanged(): return lax.all_to_all(x, 'panel', split_axis=0, concat_axis=0, tiled=True)  28.7 us
    pallas_call x4, Pallas kernels, update(): pl.pallas_call(functools.partial(update_kernel, steps, source, result, gr...  28.6 us
    ppermute x6, waiting for transfers between devices, shifted(): lax.ppermute(x, 'blk', [(i, (i + by) % length) for i in range(length)])  20.3 us
    all_to_all x4, waiting for transfers between devices, exchanged(): return lax.all_to_all(x, 'panel', split_axis=0, concat_axis=0, tiled=True)  12.5 us
    ppermute x6, starting transfers between devices, shifted(): lax.ppermute(x, 'blk', [(i, (i + by) % length) for i in range(length)])  10.9 us
    pallas_call x5, Pallas kernels, call(): pl.pallas_call(kernel, out_shape=[jax.ShapeDtypeStruct(shape, BF16) for s...  7.06 us
    unnamed x22, local copies, waits for them, and re-layouts  4.71 us
  transfers between devices with their start and end apart: 10, of which 2 were waited for; matrix products, arithmetic and copies ran while one was open for 4% of the time, Pallas kernels for 29%

profile of v1, /device:TPU:32, one launch (start us, length us, event | category | flops | bytes accessed | tf_op | source)
XLA Modules:
  0.0 119.0 jit_solution(4830500044197116705)
XLA Ops:
  0.6 1.1 copy-done
  1.8 1.4 %to_wire.1 = bf16[16,160,128]{2,1,0:T(8,128)(2,1)} custom-call(bf16[20,16128]{1,0:T(8,128)(2,1)S(1)} %bitcast.13), custom_call_target="tpu_custom_call" | custom-call | flops 2000000000 | bytes 100000 | tf_op jit(solution)/shard_map/to_wire/pallas_call | solution.py:273
  3.1 7.2 %all-to-all-start = ((bf16[16,160,128]{2,1,0:T(8,128)(2,1)}), bf16[16,160,128]{2,1,0:T(8,128)(2,1)S(1)}, u32[]{:S(2)}, u32[]{:S(2)}) async-start(bf16[16,160,128]{2,1,0:T(8,128)(2,1)} %to_wire.1), calls=%async_computation | async-start | bytes 1310720 | tf_op jit(solution)/shard_map/all_to_all | solution.py:369
  10.3 0.6 copy-done.9
  11.0 2.0 %collective-permute-start.1 = (s32[20]{0:T(128)S(1)}, s32[20]{0:T(128)S(1)}, u32[]{:S(2)}, u32[]{:S(2)}) collective-permute-start(s32[20]{0:T(128)S(1)} %get-tuple-element.16), channel_id=1, source_target_pairs={{0,16},{16,32},{32,48},{48,64},{64,80},{80,96},{96,112},{112,128},... | collective-permute-start | bytes 248 | tf_op jit(solution)/shard_map/ppermute | solution.py:365
  13.0 0.7 copy-done.8
  14.1 2.0 %collective-permute-start.2 = (bf16[20,2304]{1,0:T(8,128)(2,1)S(1)}, bf16[20,2304]{1,0:T(8,128)(2,1)S(1)}, u32[]{:S(2)}, u32[]{:S(2)}) collective-permute-start(bf16[20,2304]{1,0:T(8,128)(2,1)S(1)} %and_select_fusion.refs_1_.sites), channel_id=1, source_target_pairs={{0,16},{16,32},{32,48},{48,64},{64,80},{80,96},{96,112},{112,128},... | collective-permute-start | bytes 276488 | tf_op jit(solution)/shard_map/ppermute | solution.py:365
  16.4 0.4 multiply_bitcast_fusion.1
  16.8 0.4 copy.17
  17.3 0.3 reshape.112.refs_2_
  17.6 0.3 copy-done.1
  18.0 8.2 %update_l0.2 = bf16[16,160,128]{2,1,0:T(8,128)(2,1)S(1)} custom-call(bf16[20,16128]{1,0:T(8,128)(2,1)S(1)} %bitcast.14, bf16[20,2304]{1,0:T(8,128)(2,1)S(1)} %and_select_fusion.refs_1_.sites, bf16[224,256]{1,0:T(8,128)(2,1)S(1)} %reshape.112.refs_2_), custom_call_target="tpu_custom_call" | custom-call | flops 9200000000 | bytes 100000 | tf_op jit(solution)/shard_map/update_l0/pallas_call | solution.py:241
  26.2 3.7 %collective-permute-start.3 = (bf16[16,160,128]{2,1,0:T(8,128)(2,1)S(1)}, bf16[16,160,128]{2,1,0:T(8,128)(2,1)}, u32[]{:S(2)}, u32[]{:S(2)}) collective-permute-start(bf16[16,160,128]{2,1,0:T(8,128)(2,1)S(1)} %update_l0.2), channel_id=1, source_target_pairs={{0,32},{16,48},{32,64},{48,80},{64,96},{80,112},{96,128},{112,144}... | collective-permute-start | bytes 1966088 | tf_op jit(solution)/shard_map/ppermute | solution.py:365
  29.8 1.5 %collective-permute-start = (s32[20]{0:T(128)S(1)}, s32[20]{0:T(128)S(1)}, u32[]{:S(2)}, u32[]{:S(2)}) collective-permute-start(s32[20]{0:T(128)S(1)} %get-tuple-element.16), channel_id=1, source_target_pairs={{0,32},{16,48},{32,64},{48,80},{64,96},{80,112},{96,128},{112,144}... | collective-permute-start | bytes 248 | tf_op jit(solution)/shard_map/ppermute | solution.py:365
  32.3 2.0 %permute_pack.1 = bf16[16,256,128]{2,1,0:T(8,128)(2,1)} custom-call(s32[320]{0:T(512)S(1)} %fusion.11.order, s32[64]{0:T(128)S(1)} %pad_add_fusion.chosen, bf16[16,160,128]{2,1,0:T(8,128)(2,1)S(1)} %all-to-all-done.wire, bf16[20,2304]{1,0:T(8,128)(2,1)S(1)} %and_select_fusion.refs_1_.sites, bf16[20,2304]{1,0:T(8,128)(2,1)S(1)} %collective-permute-done.2.sites1.refs_2_), custom_call_target="tpu_custom_call" | custom-call | flops 2000000000 | bytes 100000 | tf_op jit(solution)/shard_map/permute_pack/pallas_call | solution.py:273
  34.3 7.2 %all-to-all-start.1 = ((bf16[16,256,128]{2,1,0:T(8,128)(2,1)}), bf16[16,256,128]{2,1,0:T(8,128)(2,1)S(1)}, u32[]{:S(2)}, u32[]{:S(2)}) async-start(bf16[16,256,128]{2,1,0:T(8,128)(2,1)} %permute_pack.1), calls=%async_computation.1 | async-start | bytes 2097152 | tf_op jit(solution)/shard_map/all_to_all | solution.py:369
  41.8 0.4 multiply_bitcast_fusion
  42.7 20.3 %collective-permute-done.3.value = bf16[16,160,128]{2,1,0:T(8,128)(2,1)} collective-permute-done((bf16[16,160,128]{2,1,0:T(8,128)(2,1)S(1)}, bf16[16,160,128]{2,1,0:T(8,128)(2,1)}, u32[]{:S(2)}, u32[]{:S(2)}) %collective-permute-start.3) | collective-permute-done | bytes 655392 | tf_op jit(solution)/shard_map/ppermute | solution.py:365
  63.0 0.6 touch.2.refs_4_
  63.6 0.6 fetch.1
  64.2 6.6 %all-to-all-start.2 = ((bf16[16,160,128]{2,1,0:T(8,128)(2,1)}), bf16[16,160,128]{2,1,0:T(8,128)(2,1)S(1)}, u32[]{:S(2)}, u32[]{:S(2)}) async-start(bf16[16,160,128]{2,1,0:T(8,128)(2,1)} %collective-permute-done.3.value), calls=%async_computation.2 | async-start | bytes 1310720 | tf_op jit(solution)/shard_map/all_to_all | solution.py:369
  70.8 5.7 %update_rr0.1 = bf16[10,128,128]{2,1,0:T(8,128)(2,1)S(1)} custom-call(bf16[16,256,128]{2,1,0:T(8,128)(2,1)S(1)} %all-to-all-done.1.wire.refs_0_, bf16[480,128]{1,0:T(8,128)(2,1)S(1)} %get-tuple-element.18.refs_1_, bf16[20,2304]{1,0:T(8,128)(2,1)S(1)} %collective-permute-done.2.sites1.refs_2_, bf16[256,224]{1,0:T(8,128)(2,1)S(1)} %copy.19.refs_3_, ...), custom_call_target="tpu_custom_call" | custom-call | flops 2400000000 | bytes 100000 | tf_op jit(solution)/shard_map/update_rr0/pallas_call | solution.py:241
  77.2 5.7 %update_rr2.1 = bf16[10,128,128]{2,1,0:T(8,128)(2,1)S(1)} custom-call(bf16[16,256,128]{2,1,0:T(8,128)(2,1)S(1)} %all-to-all-done.1.wire.refs_0_, bf16[480,128]{1,0:T(8,128)(2,1)S(1)} %get-tuple-element.18.refs_1_, bf16[20,2304]{1,0:T(8,128)(2,1)S(1)} %collective-permute-done.2.sites1.refs_2_, bf16[256,224]{1,0:T(8,128)(2,1)S(1)} %copy.19.refs_3_), custom_call_target="tpu_custom_call" | custom-call | flops 2400000000 | bytes 100000 | tf_op jit(solution)/shard_map/update_rr2/pallas_call | solution.py:241
  82.9 1.7 %collective-permute-start.5 = (bf16[10,128,128]{2,1,0:T(8,128)(2,1)S(1)}, bf16[10,128,128]{2,1,0:T(8,128)(2,1)S(1)}, u32[]{:S(2)}, u32[]{:S(2)}) collective-permute-start(bf16[10,128,128]{2,1,0:T(8,128)(2,1)S(1)} %update_rr2.1), channel_id=1, source_target_pairs={{0,224},{16,240},{32,0},{48,16},{64,32},{80,48},{96,64},{112,80},{... | collective-permute-start | bytes 983048 | tf_op jit(solution)/shard_map/ppermute | solution.py:365
  84.6 1.7 %permute.1 = bf16[16,160,128]{2,1,0:T(8,128)(2,1)} custom-call(s32[320]{0:T(512)S(1)} %fusion.14.order, bf16[16,160,128]{2,1,0:T(8,128)(2,1)S(1)} %all-to-all-done.2.wire), custom_call_target="tpu_custom_call" | custom-call | flops 2000000000 | bytes 100000 | tf_op jit(solution)/shard_map/permute/pallas_call | solution.py:273
  86.3 7.8 %all-to-all-start.3 = ((bf16[16,160,128]{2,1,0:T(8,128)(2,1)}), bf16[16,160,128]{2,1,0:T(8,128)(2,1)S(1)}, u32[]{:S(2)}, u32[]{:S(2)}) async-start(bf16[16,160,128]{2,1,0:T(8,128)(2,1)} %permute.1), calls=%async_computation.3 | async-start | bytes 1310720 | tf_op jit(solution)/shard_map/all_to_all | solution.py:369
  94.1 0.7 copy-done.2
  94.8 0.6 touch.3.refs_3_
  95.4 12.4 %all-to-all-done.3.refs_0_ = bf16[16,160,128]{2,1,0:T(8,128)(2,1)S(1)} async-done(((bf16[16,160,128]{2,1,0:T(8,128)(2,1)}), bf16[16,160,128]{2,1,0:T(8,128)(2,1)S(1)}, u32[]{:S(2)}, u32[]{:S(2)}) %all-to-all-start.3) | async-done | bytes 655392 | tf_op jit(solution)/shard_map/all_to_all | solution.py:369
  107.8 0.7 copy-done.5
  108.5 9.0 %update_l0.3 = bf16[20,16128]{1,0:T(8,128)(2,1)} custom-call(bf16[16,160,128]{2,1,0:T(8,128)(2,1)S(1)} %all-to-all-done.3.refs_0_, bf16[480,128]{1,0:T(8,128)(2,1)S(1)} %get-tuple-element.24.refs_1_, bf16[224,256]{1,0:T(8,128)(2,1)S(1)} %reshape.112.refs_2_, bf16[16,128]{1,0:T(8,128)(2,1)S(1)} %copy-done.5), custom_call_target="tpu_custom_call" | custom-call | flops 9200000000 | bytes 100000 | tf_op jit(solution)/shard_map/update_l0/pallas_call | solution.py:241
  117.6 1.4 %join.1 = bf16[20,16128]{1,0:T(8,128)(2,1)} custom-call(bf16[10,128,128]{2,1,0:T(8,128)(2,1)S(1)} %copy-done.3, bf16[10,128,128]{2,1,0:T(8,128)(2,1)S(1)} %collective-permute-done.5.second), custom_call_target="tpu_custom_call" | custom-call | flops 2000000000 | bytes 100000 | tf_op jit(solution)/shard_map/join/pallas_call | solution.py:273
  (60 shorter events, 3.0 us)
Async XLA Ops:
  0.6 1.1 copy-start
  3.1 10.8 %copy-start.7 = (bf16[1,20,2304]{2,1,0:T(8,128)(2,1)S(1)}, bf16[1,20,2304]{2,1,0:T(8,128)(2,1)}, u32[]{:S(2)}) copy-start(bf16[1,20,2304]{2,1,0:T(8,128)(2,1)} %param.8) | copy-start | bytes 276484
  3.1 29.2 %all-to-all-start = ((bf16[16,160,128]{2,1,0:T(8,128)(2,1)}), bf16[16,160,128]{2,1,0:T(8,128)(2,1)S(1)}, u32[]{:S(2)}, u32[]{:S(2)}) async-start(bf16[16,160,128]{2,1,0:T(8,128)(2,1)} %to_wire.1), calls=%async_computation | async-start | bytes 1310720 | tf_op jit(solution)/shard_map/all_to_all | solution.py:369
  10.3 0.7 copy-start.9
  11.0 20.4 %collective-permute-start.1 = (s32[20]{0:T(128)S(1)}, s32[20]{0:T(128)S(1)}, u32[]{:S(2)}, u32[]{:S(2)}) collective-permute-start(s32[20]{0:T(128)S(1)} %get-tuple-element.16), channel_id=1, source_target_pairs={{0,16},{16,32},{32,48},{48,64},{64,80},{80,96},{96,112},{112,128},... | collective-permute-start | bytes 248 | tf_op jit(solution)/shard_map/ppermute | solution.py:365
  13.0 0.7 copy-start.8
  13.9 2.1 %copy-start.6 = (bf16[28,28,4,4]{1,3,2,0:T(4,128)(2,1)S(1)}, bf16[28,28,4,4]{1,3,2,0:T(4,128)(2,1)}, u32[]{:S(2)}) copy-start(bf16[28,28,4,4]{1,3,2,0:T(4,128)(2,1)} %param.9) | copy-start | bytes 75268
  14.1 18.2 %collective-permute-start.2 = (bf16[20,2304]{1,0:T(8,128)(2,1)S(1)}, bf16[20,2304]{1,0:T(8,128)(2,1)S(1)}, u32[]{:S(2)}, u32[]{:S(2)}) collective-permute-start(bf16[20,2304]{1,0:T(8,128)(2,1)S(1)} %and_select_fusion.refs_1_.sites), channel_id=1, source_target_pairs={{0,16},{16,32},{32,48},{48,64},{64,80},{80,96},{96,112},{112,128},... | collective-permute-start | bytes 276488 | tf_op jit(solution)/shard_map/ppermute | solution.py:365
  16.8 1.1 copy-start.1
  26.2 36.8 %collective-permute-start.3 = (bf16[16,160,128]{2,1,0:T(8,128)(2,1)S(1)}, bf16[16,160,128]{2,1,0:T(8,128)(2,1)}, u32[]{:S(2)}, u32[]{:S(2)}) collective-permute-start(bf16[16,160,128]{2,1,0:T(8,128)(2,1)S(1)} %update_l0.2), channel_id=1, source_target_pairs={{0,32},{16,48},{32,64},{48,80},{64,96},{80,112},{96,128},{112,144}... | collective-permute-start | bytes 1966088 | tf_op jit(solution)/shard_map/ppermute | solution.py:365
  29.8 46.8 %collective-permute-start = (s32[20]{0:T(128)S(1)}, s32[20]{0:T(128)S(1)}, u32[]{:S(2)}, u32[]{:S(2)}) collective-permute-start(s32[20]{0:T(128)S(1)} %get-tuple-element.16), channel_id=1, source_target_pairs={{0,32},{16,48},{32,64},{48,80},{64,96},{80,112},{96,128},{112,144}... | collective-permute-start | bytes 248 | tf_op jit(solution)/shard_map/ppermute | solution.py:365
  34.3 29.3 %all-to-all-start.1 = ((bf16[16,256,128]{2,1,0:T(8,128)(2,1)}), bf16[16,256,128]{2,1,0:T(8,128)(2,1)S(1)}, u32[]{:S(2)}, u32[]{:S(2)}) async-start(bf16[16,256,128]{2,1,0:T(8,128)(2,1)} %permute_pack.1), calls=%async_computation.1 | async-start | bytes 2097152 | tf_op jit(solution)/shard_map/all_to_all | solution.py:369
  64.2 6.6 %copy-start.4 = (bf16[16,128]{1,0:T(8,128)(2,1)S(1)}, bf16[16,128]{1,0:T(8,128)(2,1)}, u32[]{:S(2)}) copy-start(bf16[16,128]{1,0:T(8,128)(2,1)} %touch.2.refs_4_) | copy-start | bytes 12292
  64.2 20.4 %all-to-all-start.2 = ((bf16[16,160,128]{2,1,0:T(8,128)(2,1)}), bf16[16,160,128]{2,1,0:T(8,128)(2,1)S(1)}, u32[]{:S(2)}, u32[]{:S(2)}) async-start(bf16[16,160,128]{2,1,0:T(8,128)(2,1)} %collective-permute-done.3.value), calls=%async_computation.2 | async-start | bytes 1310720 | tf_op jit(solution)/shard_map/all_to_all | solution.py:369
  76.5 17.5 %collective-permute-start.4 = (bf16[10,128,128]{2,1,0:T(8,128)(2,1)S(1)}, bf16[10,128,128]{2,1,0:T(8,128)(2,1)S(1)}, u32[]{:S(2)}, u32[]{:S(2)}) collective-permute-start(bf16[10,128,128]{2,1,0:T(8,128)(2,1)S(1)} %update_rr0.1), channel_id=1, source_target_pairs={{0,224},{16,240},{32,0},{48,16},{64,32},{80,48},{96,64},{112,80},{... | collective-permute-start | bytes 983048 | tf_op jit(solution)/shard_map/ppermute | solution.py:365
  82.9 34.7 %collective-permute-start.5 = (bf16[10,128,128]{2,1,0:T(8,128)(2,1)S(1)}, bf16[10,128,128]{2,1,0:T(8,128)(2,1)S(1)}, u32[]{:S(2)}, u32[]{:S(2)}) collective-permute-start(bf16[10,128,128]{2,1,0:T(8,128)(2,1)S(1)} %update_rr2.1), channel_id=1, source_target_pairs={{0,224},{16,240},{32,0},{48,16},{64,32},{80,48},{96,64},{112,80},{... | collective-permute-start | bytes 983048 | tf_op jit(solution)/shard_map/ppermute | solution.py:365
  86.3 21.5 %all-to-all-start.3 = ((bf16[16,160,128]{2,1,0:T(8,128)(2,1)}), bf16[16,160,128]{2,1,0:T(8,128)(2,1)S(1)}, u32[]{:S(2)}, u32[]{:S(2)}) async-start(bf16[16,160,128]{2,1,0:T(8,128)(2,1)} %permute.1), calls=%async_computation.3 | async-start | bytes 1310720 | tf_op jit(solution)/shard_map/all_to_all | solution.py:369
  94.1 0.7 copy-start.2
  107.8 0.7 copy-start.5
  108.5 9.1 %copy-start.3 = (bf16[10,128,128]{2,1,0:T(8,128)(2,1)S(1)}, bf16[10,128,128]{2,1,0:T(8,128)(2,1)}, u32[]{:S(2)}) copy-start(bf16[10,128,128]{2,1,0:T(8,128)(2,1)} %copy-done.2) | copy-start | bytes 983044

commit v2 on v1

--- a/solution.py
+++ b/solution.py
@@ -14,6 +14,7 @@
 LANES = 128
 TILES = 144
 ENV = WD * BLK * BLK
+SITE = PHYS * BLK * BLK
 F32, BF16 = jnp.float32, jnp.bfloat16
 
 
@@ -122,15 +123,29 @@
     return jnp.concatenate(parts, 0)
 
 
-def left_step(rows, rows_a, spread_a, operator, middle):
+def widen(operator, wide, held):
+    held[...] = jnp.zeros((2 * WD * 8, LANES), F32)
+    for t in range(PHYS):
+        value = operator[pl.ds(t, WD, stride=PHYS), :]
+        for i in range(2):
+            held[pl.ds(WD * 8 * i + PHYS * i + t, WD, stride=8), :] = value
+    wide[...] = jnp.concatenate([held[:WD * 8, :], held[WD * 8:, :]], 1).astype(BF16)
+
+
+def left_step(rows, rows_a, spread_a, operator, middle, spread):
     diag = jnp.concatenate([diagonal(rows_a, s) for s in range(PHYS)], 1).astype(BF16)
     last = spread_a[...].T.astype(BF16)
+    env = jnp.concatenate([rows[pl.ds(d, WPAD, stride=BLK), :] for d in range(BLK)], 0).astype(BF16)
+    xs = jnp.dot(env, diag, preferred_element_type=F32).astype(BF16)
     for p in range(6):
-        env = jnp.concatenate([rows[pl.ds(4 * p + d, WPAD, stride=BLK), :] for d in range(4)], 0).astype(BF16)
-        x = jnp.dot(env, diag, preferred_element_type=F32).astype(BF16)
-        x = jnp.concatenate(
-            [jnp.concatenate([x[:64, s * LANES:(s + 1) * LANES], x[64:, s * LANES:(s + 1) * LANES]], 1) for s in range(PHYS)], 0)
-        y = jnp.dot(operator[...], x, preferred_element_type=F32)
+        x = xs[128 * p:128 * p + 128]
+        for n in range(2):
+            for s in range(PHYS):
+                at = (4 * n + s) * WPAD
+                spread[p, at:at + WPAD, :LANES] = x[n * WPAD:(n + 1) * WPAD, s * LANES:(s + 1) * LANES]
+                spread[p, at:at + WPAD, LANES:] = x[64 + n * WPAD:64 + (n + 1) * WPAD, s * LANES:(s + 1) * LANES]
+    for p in range(6):
+        y = jnp.dot(operator[...], spread[p], preferred_element_type=F32)
         even = y[:, :LANES].reshape(WD, 8, LANES)
         odd = y[:, LANES:].reshape(WD, 8, LANES)
         middle[:, 16 * p:16 * p + 16, :] = jnp.concatenate([even, odd], 1).astype(BF16)
@@ -146,7 +161,7 @@
             rows[(2 * u + h) * BLK:(2 * u + h + 1) * BLK, :] = acc
 
 
-def right_step(rows, rows_a, spread_a, operator, middle):
+def right_step(rows, rows_a, spread_a, operator, middle, spread):
     first = spread_a[...].astype(BF16)
     diag = jnp.concatenate([diagonal(rows_a, s).T for s in range(PHYS)], 0).astype(BF16)
     lane = lane_ids(BLK)
@@ -164,11 +179,12 @@
     for p in range(6):
         z = jnp.concatenate([middle[2 * p], middle[2 * p + 1]], 1)
         v = jnp.dot(operator[...], z, preferred_element_type=F32).astype(BF16)
-        v = jnp.concatenate(
-            [jnp.concatenate([v[64 * t:64 * t + 64, h * LANES:(h + 1) * LANES] for t in range(PHYS)], 1) for h in range(2)], 0)
-        out = jnp.dot(v, diag, preferred_element_type=F32)
-        for d in range(4):
-            rows[pl.ds(4 * p + d, WPAD, stride=BLK), :] = out[d * WPAD:(d + 1) * WPAD, :]
+        for h in range(2):
+            for t in range(PHYS):
+                spread[LANES * p + 64 * h:LANES * p + 64 * h + 64, t * LANES:(t + 1) * LANES] = v[64 * t:64 * t + 64, h * LANES:(h + 1) * LANES]
+    out = jnp.dot(spread[...], diag, preferred_element_type=F32)
+    for d in range(BLK):
+        rows[pl.ds(d, WPAD, stride=BLK), :] = out[d * WPAD:(d + 1) * WPAD, :]
 
 
 def load_sites(site, block):
@@ -197,11 +213,15 @@
         part[m] = tiles[at:at + LANES, :].astype(BF16)
 
 
-def update_kernel(steps, source, result, groups, count, *refs):
+def update_kernel(steps, source, result, groups, count, noted, *refs):
     env, sites, operator = refs[0], refs[1:1 + len(steps)], refs[1 + len(steps)]
+    note = refs[2 + len(steps)] if noted else None
     refs = refs[count:]
     out, tiles, rows, rows_a, spread_a, middle = refs[:6]
-    blocks = refs[6:]
+    blocks = refs[6:6 + len(sites)]
+    if steps[0] == "L":
+        widen(operator, *refs[7 + len(sites):])
+        operator = refs[7 + len(sites)]
     if source != "rows":
         clear_tails(tiles)
         (load_raw if source == "raw" else load_wire)(env, tiles, *([ENV // LANES] if source == "raw" else []))
@@ -218,7 +238,7 @@
             flat_to_rows(tiles, group, 48, rows)
         for step, block in zip(steps, blocks):
             site_rows(block, group, rows_a, spread_a)
-            (left_step if step == "L" else right_step)(rows, rows_a, spread_a, operator, middle)
+            (left_step if step == "L" else right_step)(rows, rows_a, spread_a, operator, middle, refs[6 + len(sites)])
         if result == "rows":
             out[local] = rows[:WD * BLK, :].astype(BF16)
         else:
@@ -231,17 +251,19 @@
     elif result == "raw":
         store_raw(tiles, out, ENV // LANES)
     elif result == "wire":
+        if noted:
+            tiles[pl.ds(126, SEC, stride=TILES), :] = note[...].astype(F32)
         store_wire(tiles, out)
 
 
-def update(steps, source, result, groups, env, sites, operator, *tickets):
+def update(steps, source, result, groups, env, sites, operator, note=None, *tickets):
     shape = {"rows": (groups[1], WD * BLK, LANES), "part": (GRP * groups[1], LANES, LANES), "wire": (16, 160, LANES), "raw": (SEC, ENV)}[result]
     middle = (WD, 96, LANES) if steps[0] == "L" else (12, 224, LANES)
-    inputs = [env, *sites, operator, *tickets]
+    inputs = [env, *sites, operator] + ([] if note is None else [note]) + list(tickets)
     return pl.pallas_call(
-        functools.partial(update_kernel, steps, source, result, groups, len(inputs)),
+        functools.partial(update_kernel, steps, source, result, groups, len(inputs), note is not None),
         out_shape=jax.ShapeDtypeStruct(shape, BF16),
-        in_specs=[pl.BlockSpec(memory_space=pltpu.VMEM)] * (2 + len(sites)) + [pl.BlockSpec(memory_space=pl.ANY)] * len(tickets),
+        in_specs=[pl.BlockSpec(memory_space=pltpu.VMEM)] * (len(inputs) - len(tickets)) + [pl.BlockSpec(memory_space=pl.ANY)] * len(tickets),
         out_specs=pl.BlockSpec(memory_space=pltpu.VMEM),
         scratch_shapes=[
             pltpu.VMEM((SEC * TILES, LANES), F32),
@@ -249,17 +271,17 @@
             pltpu.VMEM((LANES, LANES), F32),
             pltpu.VMEM((PHYS * BLK, LANES), F32),
             pltpu.VMEM(middle, BF16),
-        ] + [pltpu.VMEM((SEC * 24, LANES), F32)] * len(sites),
-        compiler_params=pltpu.CompilerParams(vmem_limit_bytes=32 * 1024 * 1024),
-        cost_estimate=pl.CostEstimate(flops=(2300000000 if steps[0] == "L" else 600000000) * groups[1] * len(sites), bytes_accessed=100000, transcendentals=0),
+        ] + [pltpu.VMEM((SEC * 24, LANES), F32)] * len(sites)
+        + ([pltpu.VMEM((6, 256, 256), BF16), pltpu.VMEM((WD * 8, 2 * LANES), BF16), pltpu.VMEM((2 * WD * 8, LANES), F32)]
+           if steps[0] == "L" else [pltpu.VMEM((WPAD * BLK, 4 * LANES), BF16)]),
+        compiler_params=pltpu.CompilerParams(vmem_limit_bytes=16 * 1024 * 1024),
+        cost_estimate=pl.CostEstimate(flops=(2000000000 if steps[0] == "L" else 50000000) * groups[1] * len(sites), bytes_accessed=100000, transcendentals=0),
         name="update_" + "".join(steps).lower() + str(groups[0]),
     )(*inputs)
 
 
 def left_operator(op):
-    same = jnp.eye(2, dtype=BF16)
-    wide = jnp.pad(op, ((0, WPAD - WD), (0, 0), (0, 0), (0, 0)))
-    return jnp.einsum("wvts,ab->vatsbw", wide, same).reshape(WD * 8, 8 * WPAD)
+    return jnp.pad(op.transpose(1, 2, 3, 0), ((0, 0), (0, 0), (0, 0), (0, WPAD - WD))).reshape(WD * PHYS, LANES).astype(F32)
 
 
 def right_operator(op):
@@ -276,7 +298,7 @@
         in_specs=[pl.BlockSpec(memory_space=space) for space in spaces],
         out_specs=[pl.BlockSpec(memory_space=pltpu.VMEM)] * len(shapes),
         scratch_shapes=scratch,
-        compiler_params=pltpu.CompilerParams(vmem_limit_bytes=32 * 1024 * 1024),
+        compiler_params=pltpu.CompilerParams(vmem_limit_bytes=16 * 1024 * 1024),
         cost_estimate=pl.CostEstimate(flops=2000000000, bytes_accessed=100000, transcendentals=0),
         name=name,
     )(*inputs)
@@ -406,10 +428,13 @@
     return jnp.concatenate(chosen), jnp.concatenate([(me + c1) % 16 * 4 + rank, back])
 
 
-def masked(tensor, rows, cols):
-    place = jnp.arange(tensor.shape[1])
-    keep = ((place // BLK % BLK)[None, :] < rows[:, None]) & ((place % BLK)[None, :] < cols[:, None])
-    return jnp.where(keep, tensor, jnp.zeros((), BF16))
+def masked(tensor, rows, cols, noted):
+    place = jnp.arange(tensor.shape[1] + LANES)
+    live = place < tensor.shape[1]
+    keep = live & ((place // BLK % BLK)[None, :] < rows[:, None]) & ((place % BLK)[None, :] < cols[:, None])
+    tensor = jnp.pad(tensor, ((0, 0), (0, LANES)))
+    extra = jnp.where(place == SITE, (noted // SEC)[:, None], jnp.where(place == SITE + 1, (noted % SEC)[:, None], 0))
+    return jnp.where(keep, tensor, extra.astype(BF16))
 
 
 def body(left_env, right_env, site_tensors, chain_operator, targets, sector_dims):
@@ -417,17 +442,17 @@
     wire = to_wire(right_env[0])
     arrived = exchanged(wire)
 
-    target = after(targets[0], wire)
+    target = targets[0]
     code = (target // SEC - me) % 16 * SEC + target % SEC
     rows = lax.dynamic_slice_in_dim(sector_dims, me * SEC, SEC)
-    blocks = masked(site_tensors[0], rows, pick(sector_dims, target))
+    blocks = after(masked(site_tensors[0], rows, pick(sector_dims, target), code), wire)
+    blocks1 = shifted(blocks, 1)
     operator = left_operator(after(chain_operator, wire))
-    left = update(("L",), "raw", "wire", WHOLE, left_env[0], [blocks], operator)
+    left = update(("L",), "raw", "wire", WHOLE, left_env[0], [blocks], operator, blocks[:, SITE:])
     left_moved = shifted(left, 2)
-    code1, blocks1 = shifted(code, 1), shifted(blocks, 1)
-    code2 = shifted(after(code, left), 2)
-
-    c0, s0, c1, s1 = code // SEC, code % SEC, code1 // SEC, code1 % SEC
+
+    noted = blocks1[:, SITE:SITE + 2].astype(jnp.int32)
+    c0, s0, c1, s1 = code // SEC, code % SEC, noted[:, 0], noted[:, 1]
     chosen, places = move_plan(me, c1, s1)
     wire = permute_pack(right_order(c0, s0, c1, s1), chosen, after(arrived, left), blocks, blocks1)
     right = exchanged(wire)
@@ -435,14 +460,14 @@
 
     operator_r = right_operator(after(chain_operator, wire))
     left = exchanged(after(left_moved, fetched))
-    right0 = update(("R", "R"), "wire", "part", FIRST, right, [fetched, blocks1], operator_r, touch(left_moved))
+    right0 = update(("R", "R"), "wire", "part", FIRST, right, [fetched, blocks1], operator_r, None, touch(left_moved))
     right0_moved = shifted(right0, -2)
-    right1 = update(("R", "R"), "wire", "part", SECOND, after(right, right0), [fetched, blocks1], operator_r)
+    noted = after(left_moved, fetched)[15].reshape(SEC, 8, LANES)[:, 6, :2].astype(jnp.int32)
+    ordered = permute(left_order(c1, s1, noted[:, 0], noted[:, 1]), left)
+    left = exchanged(ordered)
+    right1 = update(("R", "R"), "wire", "part", SECOND, after(right, right0, ordered), [fetched, blocks1], operator_r)
     right1_moved = shifted(right1, -2)
-    code2 = after(code2, right0)
-    c2, s2 = code2 // SEC, code2 % SEC
-    left = exchanged(permute(left_order(c1, s1, c2, s2), after(left, right1)))
-    left_out = update(("L",), "wire", "raw", WHOLE, left, [pushed], operator, touch(right0_moved))
+    left_out = update(("L",), "wire", "raw", WHOLE, left, [pushed], operator, None, touch(after(right0_moved, right1)))
     right_out = join(after(right0_moved, left_out), right1_moved)
     return left_out[None], right_out[None]
 

time: 120 us -> 108 us (0.900)
  starting transfers between devices: 39.6 us -> 29.3 us
  Pallas kernels: 36.9 us -> 32.3 us
  waiting for transfers between devices: 32.8 us -> 36.7 us
    all_to_all x4, starting transfers between devices: 28.7 us -> 22.5 us  [exchanged(): return lax.all_to_all(x, 'panel', split_axis=0, concat_axis=0, tiled=True)]
    pallas_call x4, Pallas kernels: 28.6 us -> 24 us  [update(): pl.pallas_call(functools.partial(update_kernel, steps, source, result, gr...]
    ppermute x6 -> x4, starting transfers between devices: 10.9 us -> 6.72 us  [shifted(): lax.ppermute(x, 'blk', [(i, (i + by) % length) for i in range(length)])]
    all_to_all x4, waiting for transfers between devices: 12.5 us -> 14.7 us  [exchanged(): return lax.all_to_all(x, 'panel', split_axis=0, concat_axis=0, tiled=True)]
    ppermute x6 -> x4, waiting for transfers between devices: 20.3 us -> 22 us  [shifted(): lax.ppermute(x, 'blk', [(i, (i + by) % length) for i in range(length)])]
    unnamed x22, local copies, waits for them, and re-layouts: 4.71 us -> 3.49 us
  transfers between devices with their start and end apart: 10 -> 8, of which waited for: 2 -> 6; matrix products, arithmetic and copies ran while one was open for 4% -> 4% of each run, Pallas kernels for 29% -> 27%
where the time goes in v2:
time: 108 us; the launch traced here: 107 us
  waiting for transfers between devices  36.7 us (34%)
  Pallas kernels  32.3 us (30%)
  starting transfers between devices  29.3 us (27%)
  local copies, waits for them, and re-layouts  5.79 us (5%)
  other arithmetic  2.04 us (2%)
    pallas_call x4, Pallas kernels, update(): pl.pallas_call(functools.partial(update_kernel, steps, source, result, gr...  24 us
    all_to_all x4, starting transfers between devices, exchanged(): return lax.all_to_all(x, 'panel', split_axis=0, concat_axis=0, tiled=True)  22.5 us
    ppermute x4, waiting for transfers between devices, shifted(): lax.ppermute(x, 'blk', [(i, (i + by) % length) for i in range(length)])  22 us
    all_to_all x4, waiting for transfers between devices, exchanged(): return lax.all_to_all(x, 'panel', split_axis=0, concat_axis=0, tiled=True)  14.7 us
    pallas_call x5, Pallas kernels, call(): pl.pallas_call(kernel, out_shape=[jax.ShapeDtypeStruct(shape, BF16) for s...  7.08 us
    ppermute x4, starting transfers between devices, shifted(): lax.ppermute(x, 'blk', [(i, (i + by) % length) for i in range(length)])  6.72 us
    unnamed x22, local copies, waits for them, and re-layouts  3.49 us
  transfers between devices with their start and end apart: 8, of which 6 were waited for; matrix products, arithmetic and copies ran while one was open for 4% of the time, Pallas kernels for 27%

profile of v2, /device:TPU:32, one launch (start us, length us, event | category | flops | bytes accessed | tf_op | source)
XLA Modules:
  0.0 107.0 jit_solution(18379714676859547020)
XLA Ops:
  0.6 1.1 %copy-done.1 = bf16[1,20,16128]{2,1,0:T(8,128)(2,1)S(1)} copy-done((bf16[1,20,16128]{2,1,0:T(8,128)(2,1)S(1)}, bf16[1,20,16128]{2,1,0:T(8,128)(2,1)}, u32[]{:S(2)}) %copy-start.1) | copy-done | bytes 645144
  1.8 1.4 %to_wire.1 = bf16[16,160,128]{2,1,0:T(8,128)(2,1)} custom-call(bf16[20,16128]{1,0:T(8,128)(2,1)S(1)} %bitcast.26), custom_call_target="tpu_custom_call" | custom-call | flops 2000000000 | bytes 100000 | tf_op jit(solution)/shard_map/to_wire/pallas_call | solution.py:295
  3.1 7.2 %all-to-all-start = ((bf16[16,160,128]{2,1,0:T(8,128)(2,1)}), bf16[16,160,128]{2,1,0:T(8,128)(2,1)S(1)}, u32[]{:S(2)}, u32[]{:S(2)}) async-start(bf16[16,160,128]{2,1,0:T(8,128)(2,1)} %to_wire.1), calls=%async_computation | async-start | bytes 1310720 | tf_op jit(solution)/shard_map/all_to_all | solution.py:391
  10.9 2.0 %collective-permute-start.1 = (bf16[20,2432]{1,0:T(8,128)(2,1)S(1)}, bf16[20,2432]{1,0:T(8,128)(2,1)S(1)}, u32[]{:S(2)}, u32[]{:S(2)}) collective-permute-start(bf16[20,2432]{1,0:T(8,128)(2,1)S(1)} %and_select_fusion.refs_1_.sites), channel_id=1, source_target_pairs={{0,16},{16,32},{32,48},{48,64},{64,80},{80,96},{96,112},{112,128},... | collective-permute-start | bytes 291848 | tf_op jit(solution)/shard_map/ppermute | solution.py:387
  12.9 0.2 copy.21
  13.4 6.1 %update_l0.2 = bf16[16,160,128]{2,1,0:T(8,128)(2,1)S(1)} custom-call(bf16[20,16128]{1,0:T(8,128)(2,1)S(1)} %bitcast.27, bf16[20,2432]{1,0:T(8,128)(2,1)S(1)} %and_select_fusion.refs_1_.sites, f32[112,128]{1,0:T(8,128)S(1)} %reshape.201.refs_2_, bf16[20,128]{1,0:T(8,128)(2,1)S(1)} %slice.24.refs_3_), custom_call_target="tpu_custom_call" | custom-call | flops 8000000000 | bytes 100000 | tf_op jit(solution)/shard_map/update_l0/pallas_call | solution.py:263
  19.5 4.6 %collective-permute-start = (bf16[16,160,128]{2,1,0:T(8,128)(2,1)S(1)}, bf16[16,160,128]{2,1,0:T(8,128)(2,1)}, u32[]{:S(2)}, u32[]{:S(2)}) collective-permute-start(bf16[16,160,128]{2,1,0:T(8,128)(2,1)S(1)} %update_l0.2), channel_id=1, source_target_pairs={{0,32},{16,48},{32,64},{48,80},{64,96},{80,112},{96,128},{112,144}... | collective-permute-start | bytes 1966088 | tf_op jit(solution)/shard_map/ppermute | solution.py:387
  25.2 2.0 %permute_pack.1 = bf16[16,256,128]{2,1,0:T(8,128)(2,1)} custom-call(s32[320]{0:T(512)S(1)} %fusion.11.order, s32[64]{0:T(128)S(1)} %pad_add_fusion.1.chosen, bf16[16,160,128]{2,1,0:T(8,128)(2,1)S(1)} %all-to-all-done.wire, bf16[20,2432]{1,0:T(8,128)(2,1)S(1)} %and_select_fusion.refs_1_.sites, bf16[20,2432]{1,0:T(8,128)(2,1)S(1)} %collective-permute-done.1.sites1.refs_2_), custom_call_target="tpu_custom_call" | custom-call | flops 2000000000 | bytes 100000 | tf_op jit(solution)/shard_map/permute_pack/pallas_call | solution.py:295
  27.2 7.2 %all-to-all-start.1 = ((bf16[16,256,128]{2,1,0:T(8,128)(2,1)}), bf16[16,256,128]{2,1,0:T(8,128)(2,1)S(1)}, u32[]{:S(2)}, u32[]{:S(2)}) async-start(bf16[16,256,128]{2,1,0:T(8,128)(2,1)} %permute_pack.1), calls=%async_computation.1 | async-start | bytes 2097152 | tf_op jit(solution)/shard_map/all_to_all | solution.py:391
  34.5 0.2 copy.27
  34.8 0.4 multiply_bitcast_fusion
  35.2 0.3 reshape.200
  35.6 21.0 %collective-permute-done.value = bf16[16,160,128]{2,1,0:T(8,128)(2,1)} collective-permute-done((bf16[16,160,128]{2,1,0:T(8,128)(2,1)S(1)}, bf16[16,160,128]{2,1,0:T(8,128)(2,1)}, u32[]{:S(2)}, u32[]{:S(2)}) %collective-permute-start) | collective-permute-done | bytes 655392 | tf_op jit(solution)/shard_map/ppermute | solution.py:387
  56.6 0.6 touch.2.refs_4_
  57.2 2.6 %all-to-all-done.1.wire.refs_0_ = bf16[16,256,128]{2,1,0:T(8,128)(2,1)S(1)} async-done(((bf16[16,256,128]{2,1,0:T(8,128)(2,1)}), bf16[16,256,128]{2,1,0:T(8,128)(2,1)S(1)}, u32[]{:S(2)}, u32[]{:S(2)}) %all-to-all-start.1) | async-done | bytes 1048608 | tf_op jit(solution)/shard_map/all_to_all | solution.py:391
  59.8 0.6 fetch.1
  60.4 4.4 %all-to-all-start.2 = ((bf16[16,160,128]{2,1,0:T(8,128)(2,1)}), bf16[16,160,128]{2,1,0:T(8,128)(2,1)S(1)}, u32[]{:S(2)}, u32[]{:S(2)}) async-start(bf16[16,160,128]{2,1,0:T(8,128)(2,1)} %collective-permute-done.value), calls=%async_computation.2 | async-start | bytes 1310720 | tf_op jit(solution)/shard_map/all_to_all | solution.py:391
  64.8 0.8 slice_bitcast_fusion
  66.2 0.6 copy-done
  66.8 5.5 %update_rr0.1 = bf16[10,128,128]{2,1,0:T(8,128)(2,1)S(1)} custom-call(bf16[16,256,128]{2,1,0:T(8,128)(2,1)S(1)} %all-to-all-done.1.wire.refs_0_, bf16[480,128]{1,0:T(8,128)(2,1)S(1)} %get-tuple-element.15.refs_1_, bf16[20,2432]{1,0:T(8,128)(2,1)S(1)} %collective-permute-done.1.sites1.refs_2_, bf16[256,224]{1,0:T(8,128)(2,1)S(1)} %copy.24.refs_3_, ...), custom_call_target="tpu_custom_call" | custom-call | flops 200000000 | bytes 100000 | tf_op jit(solution)/shard_map/update_rr0/pallas_call | solution.py:263
  72.4 6.1 %all-to-all-done.2.wire = bf16[16,160,128]{2,1,0:T(8,128)(2,1)S(1)} async-done(((bf16[16,160,128]{2,1,0:T(8,128)(2,1)}), bf16[16,160,128]{2,1,0:T(8,128)(2,1)S(1)}, u32[]{:S(2)}, u32[]{:S(2)}) %all-to-all-start.2) | async-done | bytes 655392 | tf_op jit(solution)/shard_map/all_to_all | solution.py:391
  78.6 1.7 %permute.1 = bf16[16,160,128]{2,1,0:T(8,128)(2,1)} custom-call(s32[320]{0:T(512)S(1)} %fusion.14.order, bf16[16,160,128]{2,1,0:T(8,128)(2,1)S(1)} %all-to-all-done.2.wire), custom_call_target="tpu_custom_call" | custom-call | flops 2000000000 | bytes 100000 | tf_op jit(solution)/shard_map/permute/pallas_call | solution.py:295
  80.3 3.8 %all-to-all-start.3 = ((bf16[16,160,128]{2,1,0:T(8,128)(2,1)}), bf16[16,160,128]{2,1,0:T(8,128)(2,1)S(1)}, u32[]{:S(2)}, u32[]{:S(2)}) async-start(bf16[16,160,128]{2,1,0:T(8,128)(2,1)} %permute.1), calls=%async_computation.3 | async-start | bytes 1310720 | tf_op jit(solution)/shard_map/all_to_all | solution.py:391
  84.1 5.5 %update_rr2.1 = bf16[10,128,128]{2,1,0:T(8,128)(2,1)S(1)} custom-call(bf16[16,256,128]{2,1,0:T(8,128)(2,1)S(1)} %all-to-all-done.1.wire.refs_0_, bf16[480,128]{1,0:T(8,128)(2,1)S(1)} %get-tuple-element.15.refs_1_, bf16[20,2432]{1,0:T(8,128)(2,1)S(1)} %collective-permute-done.1.sites1.refs_2_, bf16[256,224]{1,0:T(8,128)(2,1)S(1)} %copy.24.refs_3_), custom_call_target="tpu_custom_call" | custom-call | flops 200000000 | bytes 100000 | tf_op jit(solution)/shard_map/update_rr2/pallas_call | solution.py:263
  89.7 0.7 collective-permute-done.2.value.first
  90.3 0.7 copy-done.3
  91.0 0.6 touch.3.refs_3_
  91.6 6.0 %all-to-all-done.3.refs_0_ = bf16[16,160,128]{2,1,0:T(8,128)(2,1)S(1)} async-done(((bf16[16,160,128]{2,1,0:T(8,128)(2,1)}), bf16[16,160,128]{2,1,0:T(8,128)(2,1)S(1)}, u32[]{:S(2)}, u32[]{:S(2)}) %all-to-all-start.3) | async-done | bytes 655392 | tf_op jit(solution)/shard_map/all_to_all | solution.py:391
  97.6 0.7 copy-done.5
  98.3 6.9 %update_l0.3 = bf16[20,16128]{1,0:T(8,128)(2,1)} custom-call(bf16[16,160,128]{2,1,0:T(8,128)(2,1)S(1)} %all-to-all-done.3.refs_0_, bf16[480,128]{1,0:T(8,128)(2,1)S(1)} %get-tuple-element.17.refs_1_, f32[112,128]{1,0:T(8,128)S(1)} %reshape.201.refs_2_, bf16[16,128]{1,0:T(8,128)(2,1)S(1)} %copy-done.5), custom_call_target="tpu_custom_call" | custom-call | flops 8000000000 | bytes 100000 | tf_op jit(solution)/shard_map/update_l0/pallas_call | solution.py:263
  105.2 0.4 collective-permute-done.3.second
  105.7 1.4 %join.1 = bf16[20,16128]{1,0:T(8,128)(2,1)} custom-call(bf16[10,128,128]{2,1,0:T(8,128)(2,1)S(1)} %copy-done.4, bf16[10,128,128]{2,1,0:T(8,128)(2,1)S(1)} %collective-permute-done.3.second), custom_call_target="tpu_custom_call" | custom-call | flops 2000000000 | bytes 100000 | tf_op jit(solution)/shard_map/join/pallas_call | solution.py:295
  (64 shorter events, 2.9 us)
Async XLA Ops:
  0.6 1.1 %copy-start.1 = (bf16[1,20,16128]{2,1,0:T(8,128)(2,1)S(1)}, bf16[1,20,16128]{2,1,0:T(8,128)(2,1)}, u32[]{:S(2)}) copy-start(bf16[1,20,16128]{2,1,0:T(8,128)(2,1)} %param.7) | copy-start | bytes 1935364
  3.1 7.3 %copy-start.8 = (s32[1,20]{1,0:T(1,128)S(1)}, s32[1,20]{1,0:T(1,128)}, u32[]{:S(2)}) copy-start(s32[1,20]{1,0:T(1,128)} %param.10) | copy-start | bytes 244
  3.1 7.3 %copy-start.9 = (s32[320]{0:T(512)S(1)}, s32[320]{0:T(512)}, u32[]{:S(2)}) copy-start(s32[320]{0:T(512)} %param.11) | copy-start | bytes 3844
  3.1 7.6 %copy-start.7 = (bf16[1,20,2304]{2,1,0:T(8,128)(2,1)S(1)}, bf16[1,20,2304]{2,1,0:T(8,128)(2,1)}, u32[]{:S(2)}) copy-start(bf16[1,20,2304]{2,1,0:T(8,128)(2,1)} %param.8) | copy-start | bytes 276484
  3.1 9.8 %copy-start.6 = (bf16[28,28,4,4]{1,3,2,0:T(4,128)(2,1)S(1)}, bf16[28,28,4,4]{1,3,2,0:T(4,128)(2,1)}, u32[]{:S(2)}) copy-start(bf16[28,28,4,4]{1,3,2,0:T(4,128)(2,1)} %param.9) | copy-start | bytes 75268
  3.1 22.1 %all-to-all-start = ((bf16[16,160,128]{2,1,0:T(8,128)(2,1)}), bf16[16,160,128]{2,1,0:T(8,128)(2,1)S(1)}, u32[]{:S(2)}, u32[]{:S(2)}) async-start(bf16[16,160,128]{2,1,0:T(8,128)(2,1)} %to_wire.1), calls=%async_computation | async-start | bytes 1310720 | tf_op jit(solution)/shard_map/all_to_all | solution.py:391
  10.3 3.1 %copy-start.2 = (bf16[1,20,16128]{2,1,0:T(8,128)(2,1)S(1)}, bf16[1,20,16128]{2,1,0:T(8,128)(2,1)}, u32[]{:S(2)}) copy-start(bf16[1,20,16128]{2,1,0:T(8,128)(2,1)} %param.6) | copy-start | bytes 1935364
  10.9 13.2 %collective-permute-start.1 = (bf16[20,2432]{1,0:T(8,128)(2,1)S(1)}, bf16[20,2432]{1,0:T(8,128)(2,1)S(1)}, u32[]{:S(2)}, u32[]{:S(2)}) collective-permute-start(bf16[20,2432]{1,0:T(8,128)(2,1)S(1)} %and_select_fusion.refs_1_.sites), channel_id=1, source_target_pairs={{0,16},{16,32},{32,48},{48,64},{64,80},{80,96},{96,112},{112,128},... | collective-permute-start | bytes 291848 | tf_op jit(solution)/shard_map/ppermute | solution.py:387
  19.5 37.1 %collective-permute-start = (bf16[16,160,128]{2,1,0:T(8,128)(2,1)S(1)}, bf16[16,160,128]{2,1,0:T(8,128)(2,1)}, u32[]{:S(2)}, u32[]{:S(2)}) collective-permute-start(bf16[16,160,128]{2,1,0:T(8,128)(2,1)S(1)} %update_l0.2), channel_id=1, source_target_pairs={{0,32},{16,48},{32,64},{48,80},{64,96},{80,112},{96,128},{112,144}... | collective-permute-start | bytes 1966088 | tf_op jit(solution)/shard_map/ppermute | solution.py:387
  27.2 32.5 %all-to-all-start.1 = ((bf16[16,256,128]{2,1,0:T(8,128)(2,1)}), bf16[16,256,128]{2,1,0:T(8,128)(2,1)S(1)}, u32[]{:S(2)}, u32[]{:S(2)}) async-start(bf16[16,256,128]{2,1,0:T(8,128)(2,1)} %permute_pack.1), calls=%async_computation.1 | async-start | bytes 2097152 | tf_op jit(solution)/shard_map/all_to_all | solution.py:391
  60.4 18.2 %all-to-all-start.2 = ((bf16[16,160,128]{2,1,0:T(8,128)(2,1)}), bf16[16,160,128]{2,1,0:T(8,128)(2,1)S(1)}, u32[]{:S(2)}, u32[]{:S(2)}) async-start(bf16[16,160,128]{2,1,0:T(8,128)(2,1)} %collective-permute-done.value), calls=%async_computation.2 | async-start | bytes 1310720 | tf_op jit(solution)/shard_map/all_to_all | solution.py:391
  66.1 0.7 copy-start
  72.3 18.0 %collective-permute-start.2 = (bf16[10,128,128]{2,1,0:T(8,128)(2,1)S(1)}, bf16[10,128,128]{2,1,0:T(8,128)(2,1)S(1)}, u32[]{:S(2)}, u32[]{:S(2)}) collective-permute-start(bf16[10,128,128]{2,1,0:T(8,128)(2,1)S(1)} %update_rr0.1), channel_id=1, source_target_pairs={{0,224},{16,240},{32,0},{48,16},{64,32},{80,48},{96,64},{112,80},{... | collective-permute-start | bytes 983048 | tf_op jit(solution)/shard_map/ppermute | solution.py:387
  80.3 17.3 %all-to-all-start.3 = ((bf16[16,160,128]{2,1,0:T(8,128)(2,1)}), bf16[16,160,128]{2,1,0:T(8,128)(2,1)S(1)}, u32[]{:S(2)}, u32[]{:S(2)}) async-start(bf16[16,160,128]{2,1,0:T(8,128)(2,1)} %permute.1), calls=%async_computation.3 | async-start | bytes 1310720 | tf_op jit(solution)/shard_map/all_to_all | solution.py:391
  89.6 16.1 %collective-permute-start.3 = (bf16[10,128,128]{2,1,0:T(8,128)(2,1)S(1)}, bf16[10,128,128]{2,1,0:T(8,128)(2,1)S(1)}, u32[]{:S(2)}, u32[]{:S(2)}) collective-permute-start(bf16[10,128,128]{2,1,0:T(8,128)(2,1)S(1)} %update_rr2.1), channel_id=1, source_target_pairs={{0,224},{16,240},{32,0},{48,16},{64,32},{80,48},{96,64},{112,80},{... | collective-permute-start | bytes 983048 | tf_op jit(solution)/shard_map/ppermute | solution.py:387
  90.3 0.7 copy-start.3
  97.6 0.7 copy-start.5
  98.3 7.4 %copy-start.4 = (bf16[10,128,128]{2,1,0:T(8,128)(2,1)S(1)}, bf16[10,128,128]{2,1,0:T(8,128)(2,1)}, u32[]{:S(2)}) copy-start(bf16[10,128,128]{2,1,0:T(8,128)(2,1)} %copy-done.3) | copy-start | bytes 983044

commit v3 on v2

--- a/solution.py
+++ b/solution.py
@@ -9,7 +9,7 @@
 WD, PHYS, BLK = 28, 4, 24
 WPAD = 32
 SEC = 20
-FIRST, SECOND, WHOLE = (0, 2), (2, 2), (0, 4)
+PIECES, WHOLE = ((0, 2), (2, 2)), (0, 4)
 GRP = 5
 LANES = 128
 TILES = 144
@@ -226,26 +226,35 @@
         clear_tails(tiles)
         (load_raw if source == "raw" else load_wire)(env, tiles, *([ENV // LANES] if source == "raw" else []))
     else:
-        rows[WD * BLK:, :] = jnp.zeros(((WPAD - WD) * BLK, LANES), F32)
+        for local in range(groups[1]):
+            rows[local, WD * BLK:, :] = jnp.zeros(((WPAD - WD) * BLK, LANES), F32)
     for site, block in zip(sites, blocks):
         load_sites(site, block)
 
-    def one(local, carry):
-        group = local + groups[0]
+    def enter(local):
         if source == "rows":
-            rows[:WD * BLK, :] = env[local].astype(F32)
+            rows.at[local][:WD * BLK, :] = env[local].astype(F32)
         else:
-            flat_to_rows(tiles, group, 48, rows)
-        for step, block in zip(steps, blocks):
-            site_rows(block, group, rows_a, spread_a)
-            (left_step if step == "L" else right_step)(rows, rows_a, spread_a, operator, middle, refs[6 + len(sites)])
+            flat_to_rows(tiles, local + groups[0], 48, rows.at[local])
+        for n, block in enumerate(blocks):
+            site_rows(block, local + groups[0], rows_a.at[local, n], spread_a.at[local, n])
+
+    def leave(local):
         if result == "rows":
-            out[local] = rows[:WD * BLK, :].astype(BF16)
+            out[local] = rows.at[local][:WD * BLK, :].astype(BF16)
         else:
-            rows_to_flat(rows, group, 48, tiles)
-        return carry
-
-    lax.fori_loop(0, groups[1], one, 0)
+            rows_to_flat(rows.at[local], local + groups[0], 48, tiles)
+
+    enter(0)
+    for local in range(groups[1]):
+        if local + 1 < groups[1]:
+            enter(local + 1)
+        for n, step in enumerate(steps):
+            (left_step if step == "L" else right_step)(
+                rows.at[local], rows_a.at[local, n], spread_a.at[local, n], operator, middle.at[local % 2], refs[6 + len(sites)])
+        if local > 0:
+            leave(local - 1)
+    leave(groups[1] - 1)
     if result == "part":
         store_part(tiles, out, groups)
     elif result == "raw":
@@ -267,10 +276,10 @@
         out_specs=pl.BlockSpec(memory_space=pltpu.VMEM),
         scratch_shapes=[
             pltpu.VMEM((SEC * TILES, LANES), F32),
-            pltpu.VMEM((WPAD * BLK, LANES), F32),
-            pltpu.VMEM((LANES, LANES), F32),
-            pltpu.VMEM((PHYS * BLK, LANES), F32),
-            pltpu.VMEM(middle, BF16),
+            pltpu.VMEM((groups[1], WPAD * BLK, LANES), F32),
+            pltpu.VMEM((groups[1], len(sites), LANES, LANES), F32),
+            pltpu.VMEM((groups[1], len(sites), PHYS * BLK, LANES), F32),
+            pltpu.VMEM((2,) + middle, BF16),
         ] + [pltpu.VMEM((SEC * 24, LANES), F32)] * len(sites)
         + ([pltpu.VMEM((6, 256, 256), BF16), pltpu.VMEM((WD * 8, 2 * LANES), BF16), pltpu.VMEM((2 * WD * 8, LANES), F32)]
            if steps[0] == "L" else [pltpu.VMEM((WPAD * BLK, 4 * LANES), BF16)]),
@@ -325,61 +334,55 @@
             out[q, 16 * m:16 * m + 16, :] = jnp.concatenate(pair, 0).astype(BF16)
 
 
-def permute_pack_kernel(order, chosen, wire, sites, sites1, out, held, block, block1):
+def permute_pack_kernel(order, chosen, wire, sites, out, held, block):
     permute_wire(order, wire, out, held)
     load_sites(sites, block)
-    load_sites(sites1, block1)
-    for q in range(16):
-        for n, source in enumerate((block, block1)):
-            pair = [source[pl.ds(pl.multiple_of(chosen[32 * n + 2 * q + h] * 24, 8), 24), :] for h in range(2)]
-            out[q, 160 + 48 * n:208 + 48 * n, :] = jnp.concatenate(pair, 0).astype(BF16)
-
-
-def permute_pack(order, chosen, wire, sites, sites1):
-    scratch = [pltpu.VMEM((16 * 160, LANES), F32)] + [pltpu.VMEM((SEC * 24, LANES), F32)] * 2
-    return call(permute_pack_kernel, "permute_pack", [(16, 256, LANES)], [order, chosen, wire, sites, sites1], scratch, 2)[0]
-
-
-def fetch_kernel(places, wire, fetched, pushed, extra):
-    for q in range(16):
-        extra[q * 96:q * 96 + 96, :] = wire[q, 160:256, :].astype(F32)
-    for n, out in enumerate((fetched, pushed)):
-        for m in range(SEC // 2):
-            pair = [extra[pl.ds(pl.multiple_of(places[SEC * n + 2 * m + h] * 24, 8), 24), :] for h in range(2)]
-            out[48 * m:48 * m + 48, :] = jnp.concatenate(pair, 0).astype(BF16)
+    for q in range(16):
+        pair = [block[pl.ds(pl.multiple_of(chosen[2 * q + h] * 24, 8), 24), :] for h in range(2)]
+        out[q, 160:208, :] = jnp.concatenate(pair, 0).astype(BF16)
+
+
+def permute_pack(order, chosen, wire, sites):
+    scratch = [pltpu.VMEM((16 * 160, LANES), F32), pltpu.VMEM((SEC * 24, LANES), F32)]
+    return call(permute_pack_kernel, "permute_pack", [(16, 208, LANES)], [order, chosen, wire, sites], scratch, 2)[0]
+
+
+def fetch_kernel(places, wire, fetched, extra):
+    for q in range(16):
+        extra[q * 48:q * 48 + 48, :] = wire[q, 160:208, :].astype(F32)
+    for m in range(SEC // 2):
+        pair = [extra[pl.ds(pl.multiple_of(places[2 * m + h] * 24, 8), 24), :] for h in range(2)]
+        fetched[48 * m:48 * m + 48, :] = jnp.concatenate(pair, 0).astype(BF16)
 
 
 def fetch(places, wire):
-    return call(fetch_kernel, "fetch", [(SEC * 24, LANES)] * 2, [places, wire], [pltpu.VMEM((16 * 96, LANES), F32)], 1)
-
-
-def touch_kernel(value, out):
-    out[...] = jnp.zeros((16, LANES), BF16)
-
-
-def touch(value):
+    return call(fetch_kernel, "fetch", [(SEC * 24, LANES)], [places, wire], [pltpu.VMEM((16 * 48, LANES), F32)], 1)[0]
+
+
+def touch_kernel(*refs):
+    refs[-1][...] = jnp.zeros((16, LANES), BF16)
+
+
+def touch(*values):
     return pl.pallas_call(
         touch_kernel,
         out_shape=jax.ShapeDtypeStruct((16, LANES), BF16),
-        in_specs=[pl.BlockSpec(memory_space=pl.ANY)],
+        in_specs=[pl.BlockSpec(memory_space=pl.ANY)] * len(values),
         out_specs=pl.BlockSpec(memory_space=pltpu.VMEM),
         cost_estimate=pl.CostEstimate(flops=20000000000, bytes_accessed=1000, transcendentals=0),
         name="touch",
-    )(value)
-
-
-def permute(order, wire):
-    return call(permute_wire, "permute", [(16, 160, LANES)], [order, wire], [pltpu.VMEM((16 * 160, LANES), F32)], 1)[0]
-
-
-def join_kernel(first, second, out, tiles):
-    load_part(first, tiles, FIRST)
-    load_part(second, tiles, SECOND)
+    )(*values)
+
+
+def join_kernel(*refs):
+    parts, out, tiles = refs[:-2], refs[-2], refs[-1]
+    for part, groups in zip(parts, PIECES):
+        load_part(part, tiles, groups)
     store_raw(tiles, out, ENV // LANES)
 
 
-def join(first, second):
-    return call(join_kernel, "join", [(SEC, ENV)], [first, second], [pltpu.VMEM((SEC * TILES, LANES), F32)])[0]
+def join(*parts):
+    return call(join_kernel, "join", [(SEC, ENV)], parts, [pltpu.VMEM((SEC * TILES, LANES), F32)])[0]
 
 
 def shifted(x, by):
@@ -424,8 +427,8 @@
     pushed = same & (((place // 2 - me) % 16)[:, None] == c1[None, :])
     chosen = [jnp.sum(jnp.where(asked, s1[None, :], 0), axis=1), jnp.sum(jnp.where(pushed, slots[None, :], 0), axis=1)]
     landing = slots[:, None] == s1[None, :]
-    back = jnp.sum(jnp.where(landing, ((me - c1) % 16 * 4 + 2 + rank)[None, :], 0), axis=1)
-    return jnp.concatenate(chosen), jnp.concatenate([(me + c1) % 16 * 4 + rank, back])
+    back = jnp.sum(jnp.where(landing, ((me - c1) % 16 * 2 + rank)[None, :], 0), axis=1)
+    return chosen, [(me + c1) % 16 * 2 + rank, back]
 
 
 def masked(tensor, rows, cols, noted):
@@ -454,21 +457,24 @@
     noted = blocks1[:, SITE:SITE + 2].astype(jnp.int32)
     c0, s0, c1, s1 = code // SEC, code % SEC, noted[:, 0], noted[:, 1]
     chosen, places = move_plan(me, c1, s1)
-    wire = permute_pack(right_order(c0, s0, c1, s1), chosen, after(arrived, left), blocks, blocks1)
+    wire = permute_pack(right_order(c0, s0, c1, s1), chosen[0], after(arrived, left), blocks)
     right = exchanged(wire)
-    fetched, pushed = fetch(places, right)
+    fetched = fetch(places[0], right)
 
     operator_r = right_operator(after(chain_operator, wire))
     left = exchanged(after(left_moved, fetched))
-    right0 = update(("R", "R"), "wire", "part", FIRST, right, [fetched, blocks1], operator_r, None, touch(left_moved))
-    right0_moved = shifted(right0, -2)
-    noted = after(left_moved, fetched)[15].reshape(SEC, 8, LANES)[:, 6, :2].astype(jnp.int32)
-    ordered = permute(left_order(c1, s1, noted[:, 0], noted[:, 1]), left)
+    def right_piece(number, *order):
+        tickets = [touch(left_moved)] if number == 0 else []
+        piece = update(("R", "R"), "wire", "part", PIECES[number], after(right, *order), [fetched, blocks1], operator_r, None, *tickets)
+        return piece, shifted(piece, -2)
+
+    right0, moved0 = right_piece(0)
+    noted = after(left_moved, right0)[15].reshape(SEC, 8, LANES)[:, 6, :2].astype(jnp.int32)
+    ordered = permute_pack(left_order(c1, s1, noted[:, 0], noted[:, 1]), chosen[1], left, blocks1)
     left = exchanged(ordered)
-    right1 = update(("R", "R"), "wire", "part", SECOND, after(right, right0, ordered), [fetched, blocks1], operator_r)
-    right1_moved = shifted(right1, -2)
-    left_out = update(("L",), "wire", "raw", WHOLE, left, [pushed], operator, None, touch(after(right0_moved, right1)))
-    right_out = join(after(right0_moved, left_out), right1_moved)
+    right1, moved1 = right_piece(1, right0, ordered)
+    left_out = update(("L",), "wire", "raw", WHOLE, left, [fetch(places[1], left)], operator, None, touch(after(moved0, right1)))
+    right_out = join(after(moved0, left_out), moved1)
     return left_out[None], right_out[None]
 
 

time: 108 us -> 107 us (level)
  starting transfers between devices: 29.3 us -> 33.2 us
  waiting for transfers between devices: 36.7 us -> 33.1 us
  Pallas kernels: 32.3 us -> 30.3 us
    ppermute x4, starting transfers between devices: 6.72 us -> 10.6 us  [shifted(): lax.ppermute(x, 'blk', [(i, (i + by) % length) for i in range(length)])]
    ppermute x4, waiting for transfers between devices: 22 us -> 19.4 us  [shifted(): lax.ppermute(x, 'blk', [(i, (i + by) % length) for i in range(length)])]
    pallas_call x4, Pallas kernels: 24 us -> 21.5 us  [update(): pl.pallas_call(functools.partial(update_kernel, steps, source, result, gr...]
    pallas_call x5 -> x6, Pallas kernels: 7.08 us -> 7.62 us  [call(): pl.pallas_call(kernel, out_shape=[jax.ShapeDtypeStruct(shape, BF16) for s...]
    unnamed x22 -> x24, local copies, waits for them, and re-layouts: 3.49 us -> 3.16 us
  transfers between devices with their start and end apart: 8 -> 8, of which waited for: 6 -> 4; matrix products, arithmetic and copies ran while one was open for 4% -> 4% of each run, Pallas kernels for 27% -> 26%
where the time goes in v3:
time: 107 us; the launch traced here: 105 us
  starting transfers between devices  33.2 us (31%)
  waiting for transfers between devices  33.1 us (31%)
  Pallas kernels  30.3 us (28%)
  local copies, waits for them, and re-layouts  5.44 us (5%)
  other arithmetic  1.9 us (2%)
    all_to_all x4, starting transfers between devices, exchanged(): return lax.all_to_all(x, 'panel', split_axis=0, concat_axis=0, tiled=True)  22.6 us
    pallas_call x4, Pallas kernels, update(): pl.pallas_call(functools.partial(update_kernel, steps, source, result, gr...  21.5 us
    ppermute x4, waiting for transfers between devices, shifted(): lax.ppermute(x, 'blk', [(i, (i + by) % length) for i in range(length)])  19.4 us
    all_to_all x4, waiting for transfers between devices, exchanged(): return lax.all_to_all(x, 'panel', split_axis=0, concat_axis=0, tiled=True)  13.8 us
    ppermute x4, starting transfers between devices, shifted(): lax.ppermute(x, 'blk', [(i, (i + by) % length) for i in range(length)])  10.6 us
    pallas_call x6, Pallas kernels, call(): pl.pallas_call(kernel, out_shape=[jax.ShapeDtypeStruct(shape, BF16) for s...  7.62 us
    unnamed x24, local copies, waits for them, and re-layouts  3.16 us
  transfers between devices with their start and end apart: 8, of which 4 were waited for; matrix products, arithmetic and copies ran while one was open for 4% of the time, Pallas kernels for 26%

profile of v3, /device:TPU:32, one launch (start us, length us, event | category | flops | bytes accessed | tf_op | source)
XLA Modules:
  0.0 105.0 jit_solution(10450781915752252013)
XLA Ops:
  0.6 1.1 %copy-done.1 = bf16[1,20,16128]{2,1,0:T(8,128)(2,1)S(1)} copy-done((bf16[1,20,16128]{2,1,0:T(8,128)(2,1)S(1)}, bf16[1,20,16128]{2,1,0:T(8,128)(2,1)}, u32[]{:S(2)}) %copy-start.1) | copy-done | bytes 645144
  1.8 1.4 %to_wire.1 = bf16[16,160,128]{2,1,0:T(8,128)(2,1)} custom-call(bf16[20,16128]{1,0:T(8,128)(2,1)S(1)} %bitcast.26), custom_call_target="tpu_custom_call" | custom-call | flops 2000000000 | bytes 100000 | tf_op jit(solution)/shard_map/to_wire/pallas_call | solution.py:304
  3.1 7.2 %all-to-all-start = ((bf16[16,160,128]{2,1,0:T(8,128)(2,1)}), bf16[16,160,128]{2,1,0:T(8,128)(2,1)S(1)}, u32[]{:S(2)}, u32[]{:S(2)}) async-start(bf16[16,160,128]{2,1,0:T(8,128)(2,1)} %to_wire.1), calls=%async_computation | async-start | bytes 1310720 | tf_op jit(solution)/shard_map/all_to_all | solution.py:394
  10.9 2.0 %collective-permute-start.1 = (bf16[20,2432]{1,0:T(8,128)(2,1)S(1)}, bf16[20,2432]{1,0:T(8,128)(2,1)S(1)}, u32[]{:S(2)}, u32[]{:S(2)}) collective-permute-start(bf16[20,2432]{1,0:T(8,128)(2,1)S(1)} %and_select_fusion.refs_1_.sites), channel_id=1, source_target_pairs={{0,16},{16,32},{32,48},{48,64},{64,80},{80,96},{96,112},{112,128},... | collective-permute-start | bytes 291848 | tf_op jit(solution)/shard_map/ppermute | solution.py:390
  12.9 0.2 copy.21
  13.4 5.4 %update_l0.2 = bf16[16,160,128]{2,1,0:T(8,128)(2,1)S(1)} custom-call(bf16[20,16128]{1,0:T(8,128)(2,1)S(1)} %bitcast.27, bf16[20,2432]{1,0:T(8,128)(2,1)S(1)} %and_select_fusion.refs_1_.sites, f32[112,128]{1,0:T(8,128)S(1)} %reshape.200.refs_2_, bf16[20,128]{1,0:T(8,128)(2,1)S(1)} %slice.24.refs_3_), custom_call_target="tpu_custom_call" | custom-call | flops 8000000000 | bytes 100000 | tf_op jit(solution)/shard_map/update_l0/pallas_call | solution.py:272
  18.8 4.6 %collective-permute-start = (bf16[16,160,128]{2,1,0:T(8,128)(2,1)S(1)}, bf16[16,160,128]{2,1,0:T(8,128)(2,1)S(1)}, u32[]{:S(2)}, u32[]{:S(2)}) collective-permute-start(bf16[16,160,128]{2,1,0:T(8,128)(2,1)S(1)} %update_l0.2), channel_id=1, source_target_pairs={{0,32},{16,48},{32,64},{48,80},{64,96},{80,112},{96,128},{112,144}... | collective-permute-start | bytes 1966088 | tf_op jit(solution)/shard_map/ppermute | solution.py:390
  24.4 1.9 %permute_pack.2 = bf16[16,208,128]{2,1,0:T(8,128)(2,1)} custom-call(s32[320]{0:T(512)S(1)} %fusion.11.order, s32[32]{0:T(128)S(1)} %get-tuple-element.23.chosen, bf16[16,160,128]{2,1,0:T(8,128)(2,1)S(1)} %all-to-all-done.wire, bf16[20,2432]{1,0:T(8,128)(2,1)S(1)} %and_select_fusion.refs_1_.sites), custom_call_target="tpu_custom_call" | custom-call | flops 2000000000 | bytes 100000 | tf_op jit(solution)/shard_map/permute_pack/pallas_call | solution.py:304
  26.2 7.2 %all-to-all-start.1 = ((bf16[16,208,128]{2,1,0:T(8,128)(2,1)}), bf16[16,208,128]{2,1,0:T(8,128)(2,1)S(1)}, u32[]{:S(2)}, u32[]{:S(2)}) async-start(bf16[16,208,128]{2,1,0:T(8,128)(2,1)} %permute_pack.2), calls=%async_computation.1 | async-start | bytes 1703936 | tf_op jit(solution)/shard_map/all_to_all | solution.py:394
  33.5 0.2 copy.27
  33.8 0.4 multiply_bitcast_fusion
  34.2 0.3 reshape.199
  34.6 19.4 %collective-permute-done.refs_0_ = bf16[16,160,128]{2,1,0:T(8,128)(2,1)S(1)} collective-permute-done((bf16[16,160,128]{2,1,0:T(8,128)(2,1)S(1)}, bf16[16,160,128]{2,1,0:T(8,128)(2,1)S(1)}, u32[]{:S(2)}, u32[]{:S(2)}) %collective-permute-start) | collective-permute-done | bytes 655392 | tf_op jit(solution)/shard_map/ppermute | solution.py:390
  54.0 0.8 copy-done.6
  54.8 0.6 touch.2.refs_4_
  55.4 1.1 all-to-all-done.1.wire.refs_0_
  56.5 0.6 fetch.2.refs_1_
  57.1 4.6 %all-to-all-start.2 = ((bf16[16,160,128]{2,1,0:T(8,128)(2,1)}), bf16[16,160,128]{2,1,0:T(8,128)(2,1)S(1)}, u32[]{:S(2)}, u32[]{:S(2)}) async-start(bf16[16,160,128]{2,1,0:T(8,128)(2,1)} %copy-done.6), calls=%async_computation.2 | async-start | bytes 1310720 | tf_op jit(solution)/shard_map/all_to_all | solution.py:394
  61.7 5.0 %update_rr0.1 = bf16[10,128,128]{2,1,0:T(8,128)(2,1)S(1)} custom-call(bf16[16,208,128]{2,1,0:T(8,128)(2,1)S(1)} %all-to-all-done.1.wire.refs_0_, bf16[480,128]{1,0:T(8,128)(2,1)S(1)} %fetch.2.refs_1_, bf16[20,2432]{1,0:T(8,128)(2,1)S(1)} %collective-permute-done.1.refs_2_.sites, bf16[256,224]{1,0:T(8,128)(2,1)S(1)} %copy.23.refs_3_, bf16[16,128]{1,0:T(8,128)(2,1)S(1)} %copy-done), custom_call_target="tpu_custom_call" | custom-call | flops 200000000 | bytes 100000 | tf_op jit(solution)/shard_map/update_rr0/pallas_call | solution.py:272
  66.7 1.9 %collective-permute-start.2 = (bf16[10,128,128]{2,1,0:T(8,128)(2,1)S(1)}, bf16[10,128,128]{2,1,0:T(8,128)(2,1)S(1)}, u32[]{:S(2)}, u32[]{:S(2)}) collective-permute-start(bf16[10,128,128]{2,1,0:T(8,128)(2,1)S(1)} %update_rr0.1), channel_id=1, source_target_pairs={{0,224},{16,240},{32,0},{48,16},{64,32},{80,48},{96,64},{112,80},{... | collective-permute-start | bytes 983048 | tf_op jit(solution)/shard_map/ppermute | solution.py:390
  68.6 0.8 slice_bitcast_fusion
  70.1 5.4 %all-to-all-done.2.wire = bf16[16,160,128]{2,1,0:T(8,128)(2,1)S(1)} async-done(((bf16[16,160,128]{2,1,0:T(8,128)(2,1)}), bf16[16,160,128]{2,1,0:T(8,128)(2,1)S(1)}, u32[]{:S(2)}, u32[]{:S(2)}) %all-to-all-start.2) | async-done | bytes 655392 | tf_op jit(solution)/shard_map/all_to_all | solution.py:394
  75.4 1.9 %permute_pack.3 = bf16[16,208,128]{2,1,0:T(8,128)(2,1)} custom-call(s32[320]{0:T(512)S(1)} %fusion.14.order, s32[32]{0:T(128)S(1)} %get-tuple-element.22.chosen, bf16[16,160,128]{2,1,0:T(8,128)(2,1)S(1)} %all-to-all-done.2.wire, bf16[20,2432]{1,0:T(8,128)(2,1)S(1)} %collective-permute-done.1.refs_2_.sites), custom_call_target="tpu_custom_call" | custom-call | flops 2000000000 | bytes 100000 | tf_op jit(solution)/shard_map/permute_pack/pallas_call | solution.py:304
  77.3 3.6 %all-to-all-start.3 = ((bf16[16,208,128]{2,1,0:T(8,128)(2,1)}), bf16[16,208,128]{2,1,0:T(8,128)(2,1)S(1)}, u32[]{:S(2)}, u32[]{:S(2)}) async-start(bf16[16,208,128]{2,1,0:T(8,128)(2,1)} %permute_pack.3), calls=%async_computation.3 | async-start | bytes 1703936 | tf_op jit(solution)/shard_map/all_to_all | solution.py:394
  80.9 5.0 %update_rr2.1 = bf16[10,128,128]{2,1,0:T(8,128)(2,1)S(1)} custom-call(bf16[16,208,128]{2,1,0:T(8,128)(2,1)S(1)} %all-to-all-done.1.wire.refs_0_, bf16[480,128]{1,0:T(8,128)(2,1)S(1)} %fetch.2.refs_1_, bf16[20,2432]{1,0:T(8,128)(2,1)S(1)} %collective-permute-done.1.refs_2_.sites, bf16[256,224]{1,0:T(8,128)(2,1)S(1)} %copy.23.refs_3_), custom_call_target="tpu_custom_call" | custom-call | flops 200000000 | bytes 100000 | tf_op jit(solution)/shard_map/update_rr2/pallas_call | solution.py:272
  85.9 2.2 %collective-permute-start.3 = (bf16[10,128,128]{2,1,0:T(8,128)(2,1)S(1)}, bf16[10,128,128]{2,1,0:T(8,128)(2,1)S(1)}, u32[]{:S(2)}, u32[]{:S(2)}) collective-permute-start(bf16[10,128,128]{2,1,0:T(8,128)(2,1)S(1)} %update_rr2.1), channel_id=1, source_target_pairs={{0,224},{16,240},{32,0},{48,16},{64,32},{80,48},{96,64},{112,80},{... | collective-permute-start | bytes 983048 | tf_op jit(solution)/shard_map/ppermute | solution.py:390
  88.1 0.7 copy-done.3
  88.8 0.6 touch.3.refs_3_
  89.4 7.3 %all-to-all-done.3.wire.refs_0_ = bf16[16,208,128]{2,1,0:T(8,128)(2,1)S(1)} async-done(((bf16[16,208,128]{2,1,0:T(8,128)(2,1)}), bf16[16,208,128]{2,1,0:T(8,128)(2,1)S(1)}, u32[]{:S(2)}, u32[]{:S(2)}) %all-to-all-start.3) | async-done | bytes 852000 | tf_op jit(solution)/shard_map/all_to_all | solution.py:394
  96.8 0.6 fetch.3.refs_1_
  97.5 6.2 %update_l0.3 = bf16[20,16128]{1,0:T(8,128)(2,1)} custom-call(bf16[16,208,128]{2,1,0:T(8,128)(2,1)S(1)} %all-to-all-done.3.wire.refs_0_, bf16[480,128]{1,0:T(8,128)(2,1)S(1)} %fetch.3.refs_1_, f32[112,128]{1,0:T(8,128)S(1)} %reshape.200.refs_2_, bf16[16,128]{1,0:T(8,128)(2,1)S(1)} %copy-done.5), custom_call_target="tpu_custom_call" | custom-call | flops 8000000000 | bytes 100000 | tf_op jit(solution)/shard_map/update_l0/pallas_call | solution.py:272
  103.6 1.4 %join.1 = bf16[20,16128]{1,0:T(8,128)(2,1)} custom-call(bf16[10,128,128]{2,1,0:T(8,128)(2,1)S(1)} %copy-done.4, bf16[10,128,128]{2,1,0:T(8,128)(2,1)S(1)} %collective-permute-done.3.refs_1_), custom_call_target="tpu_custom_call" | custom-call | flops 2000000000 | bytes 100000 | tf_op jit(solution)/shard_map/join/pallas_call | solution.py:304
  (65 shorter events, 2.6 us)
Async XLA Ops:
  0.6 1.1 %copy-start.1 = (bf16[1,20,16128]{2,1,0:T(8,128)(2,1)S(1)}, bf16[1,20,16128]{2,1,0:T(8,128)(2,1)}, u32[]{:S(2)}) copy-start(bf16[1,20,16128]{2,1,0:T(8,128)(2,1)} %param.7) | copy-start | bytes 1935364
  3.1 7.3 %copy-start.9 = (s32[1,20]{1,0:T(1,128)S(1)}, s32[1,20]{1,0:T(1,128)}, u32[]{:S(2)}) copy-start(s32[1,20]{1,0:T(1,128)} %param.10) | copy-start | bytes 244
  3.1 7.3 %copy-start.10 = (s32[320]{0:T(512)S(1)}, s32[320]{0:T(512)}, u32[]{:S(2)}) copy-start(s32[320]{0:T(512)} %param.11) | copy-start | bytes 3844
  3.1 7.6 %copy-start.8 = (bf16[1,20,2304]{2,1,0:T(8,128)(2,1)S(1)}, bf16[1,20,2304]{2,1,0:T(8,128)(2,1)}, u32[]{:S(2)}) copy-start(bf16[1,20,2304]{2,1,0:T(8,128)(2,1)} %param.8) | copy-start | bytes 276484
  3.1 9.8 %copy-start.7 = (bf16[28,28,4,4]{1,3,2,0:T(4,128)(2,1)S(1)}, bf16[28,28,4,4]{1,3,2,0:T(4,128)(2,1)}, u32[]{:S(2)}) copy-start(bf16[28,28,4,4]{1,3,2,0:T(4,128)(2,1)} %param.9) | copy-start | bytes 75268
  3.1 21.2 %all-to-all-start = ((bf16[16,160,128]{2,1,0:T(8,128)(2,1)}), bf16[16,160,128]{2,1,0:T(8,128)(2,1)S(1)}, u32[]{:S(2)}, u32[]{:S(2)}) async-start(bf16[16,160,128]{2,1,0:T(8,128)(2,1)} %to_wire.1), calls=%async_computation | async-start | bytes 1310720 | tf_op jit(solution)/shard_map/all_to_all | solution.py:394
  10.3 3.1 %copy-start.2 = (bf16[1,20,16128]{2,1,0:T(8,128)(2,1)S(1)}, bf16[1,20,16128]{2,1,0:T(8,128)(2,1)}, u32[]{:S(2)}) copy-start(bf16[1,20,16128]{2,1,0:T(8,128)(2,1)} %param.6) | copy-start | bytes 1935364
  10.9 12.5 %collective-permute-start.1 = (bf16[20,2432]{1,0:T(8,128)(2,1)S(1)}, bf16[20,2432]{1,0:T(8,128)(2,1)S(1)}, u32[]{:S(2)}, u32[]{:S(2)}) collective-permute-start(bf16[20,2432]{1,0:T(8,128)(2,1)S(1)} %and_select_fusion.refs_1_.sites), channel_id=1, source_target_pairs={{0,16},{16,32},{32,48},{48,64},{64,80},{80,96},{96,112},{112,128},... | collective-permute-start | bytes 291848 | tf_op jit(solution)/shard_map/ppermute | solution.py:390
  18.8 35.2 %collective-permute-start = (bf16[16,160,128]{2,1,0:T(8,128)(2,1)S(1)}, bf16[16,160,128]{2,1,0:T(8,128)(2,1)S(1)}, u32[]{:S(2)}, u32[]{:S(2)}) collective-permute-start(bf16[16,160,128]{2,1,0:T(8,128)(2,1)S(1)} %update_l0.2), channel_id=1, source_target_pairs={{0,32},{16,48},{32,64},{48,80},{64,96},{80,112},{96,128},{112,144}... | collective-permute-start | bytes 1966088 | tf_op jit(solution)/shard_map/ppermute | solution.py:390
  26.2 30.2 %all-to-all-start.1 = ((bf16[16,208,128]{2,1,0:T(8,128)(2,1)}), bf16[16,208,128]{2,1,0:T(8,128)(2,1)S(1)}, u32[]{:S(2)}, u32[]{:S(2)}) async-start(bf16[16,208,128]{2,1,0:T(8,128)(2,1)} %permute_pack.2), calls=%async_computation.1 | async-start | bytes 1703936 | tf_op jit(solution)/shard_map/all_to_all | solution.py:394
  54.0 0.8 copy-start.6
  57.1 4.6 %copy-start = (bf16[16,128]{1,0:T(8,128)(2,1)S(1)}, bf16[16,128]{1,0:T(8,128)(2,1)}, u32[]{:S(2)}) copy-start(bf16[16,128]{1,0:T(8,128)(2,1)} %touch.2.refs_4_) | copy-start | bytes 12292
  57.1 18.4 %all-to-all-start.2 = ((bf16[16,160,128]{2,1,0:T(8,128)(2,1)}), bf16[16,160,128]{2,1,0:T(8,128)(2,1)S(1)}, u32[]{:S(2)}, u32[]{:S(2)}) async-start(bf16[16,160,128]{2,1,0:T(8,128)(2,1)} %copy-done.6), calls=%async_computation.2 | async-start | bytes 1310720 | tf_op jit(solution)/shard_map/all_to_all | solution.py:394
  66.7 21.4 %collective-permute-start.2 = (bf16[10,128,128]{2,1,0:T(8,128)(2,1)S(1)}, bf16[10,128,128]{2,1,0:T(8,128)(2,1)S(1)}, u32[]{:S(2)}, u32[]{:S(2)}) collective-permute-start(bf16[10,128,128]{2,1,0:T(8,128)(2,1)S(1)} %update_rr0.1), channel_id=1, source_target_pairs={{0,224},{16,240},{32,0},{48,16},{64,32},{80,48},{96,64},{112,80},{... | collective-permute-start | bytes 983048 | tf_op jit(solution)/shard_map/ppermute | solution.py:390
  77.3 19.5 %all-to-all-start.3 = ((bf16[16,208,128]{2,1,0:T(8,128)(2,1)}), bf16[16,208,128]{2,1,0:T(8,128)(2,1)S(1)}, u32[]{:S(2)}, u32[]{:S(2)}) async-start(bf16[16,208,128]{2,1,0:T(8,128)(2,1)} %permute_pack.3), calls=%async_computation.3 | async-start | bytes 1703936 | tf_op jit(solution)/shard_map/all_to_all | solution.py:394
  85.9 17.7 %collective-permute-start.3 = (bf16[10,128,128]{2,1,0:T(8,128)(2,1)S(1)}, bf16[10,128,128]{2,1,0:T(8,128)(2,1)S(1)}, u32[]{:S(2)}, u32[]{:S(2)}) collective-permute-start(bf16[10,128,128]{2,1,0:T(8,128)(2,1)S(1)} %update_rr2.1), channel_id=1, source_target_pairs={{0,224},{16,240},{32,0},{48,16},{64,32},{80,48},{96,64},{112,80},{... | collective-permute-start | bytes 983048 | tf_op jit(solution)/shard_map/ppermute | solution.py:390
  88.1 0.7 copy-start.3
  96.8 0.7 copy-start.5
  97.5 6.2 %copy-start.4 = (bf16[10,128,128]{2,1,0:T(8,128)(2,1)S(1)}, bf16[10,128,128]{2,1,0:T(8,128)(2,1)}, u32[]{:S(2)}) copy-start(bf16[10,128,128]{2,1,0:T(8,128)(2,1)} %copy-done.3) | copy-start | bytes 983044

commit v4 on v3

--- a/solution.py
+++ b/solution.py
@@ -9,6 +9,7 @@
 WD, PHYS, BLK = 28, 4, 24
 WPAD = 32
 SEC = 20
+ROOM = 24
 PIECES, WHOLE = ((0, 2), (2, 2)), (0, 4)
 GRP = 5
 LANES = 128
@@ -81,13 +82,13 @@
 
 
 def load_raw(raw, tiles, count):
-    pad = tiles.shape[0] // SEC
+    pad = tiles.shape[0] // ROOM
     for n in range(count):
         tiles[pl.ds(n, SEC, stride=pad), :] = raw[:, n * LANES:(n + 1) * LANES].astype(F32)
 
 
 def store_raw(tiles, raw, count):
-    pad = tiles.shape[0] // SEC
+    pad = tiles.shape[0] // ROOM
     for n in range(count):
         raw[:, n * LANES:(n + 1) * LANES] = tiles[pl.ds(n, SEC, stride=pad), :].astype(BF16)
 
@@ -124,12 +125,12 @@
 
 
 def widen(operator, wide, held):
-    held[...] = jnp.zeros((2 * WD * 8, LANES), F32)
+    held[...] = jnp.zeros((2 * WPAD * 8, LANES), F32)
     for t in range(PHYS):
-        value = operator[pl.ds(t, WD, stride=PHYS), :]
+        value = operator[pl.ds(t, WPAD, stride=PHYS), :]
         for i in range(2):
-            held[pl.ds(WD * 8 * i + PHYS * i + t, WD, stride=8), :] = value
-    wide[...] = jnp.concatenate([held[:WD * 8, :], held[WD * 8:, :]], 1).astype(BF16)
+            held[pl.ds(WPAD * 8 * i + PHYS * i + t, WPAD, stride=8), :] = value
+    wide[...] = jnp.concatenate([held[:WD * 8, :], held[WPAD * 8:WPAD * 8 + WD * 8, :]], 1).astype(BF16)
 
 
 def left_step(rows, rows_a, spread_a, operator, middle, spread):
@@ -193,7 +194,7 @@
             block[c * 24 + 16:c * 24 + 24, :] = jnp.zeros((8, LANES), F32)
         load_raw(site, block, 18)
     else:
-        block[...] = site[...].astype(F32)
+        block[:SEC * 24, :] = site[...].astype(F32)
 
 
 def clear_tails(tiles):
@@ -275,13 +276,13 @@
         in_specs=[pl.BlockSpec(memory_space=pltpu.VMEM)] * (len(inputs) - len(tickets)) + [pl.BlockSpec(memory_space=pl.ANY)] * len(tickets),
         out_specs=pl.BlockSpec(memory_space=pltpu.VMEM),
         scratch_shapes=[
-            pltpu.VMEM((SEC * TILES, LANES), F32),
+            pltpu.VMEM((ROOM * TILES, LANES), F32),
             pltpu.VMEM((groups[1], WPAD * BLK, LANES), F32),
             pltpu.VMEM((groups[1], len(sites), LANES, LANES), F32),
             pltpu.VMEM((groups[1], len(sites), PHYS * BLK, LANES), F32),
             pltpu.VMEM((2,) + middle, BF16),
-        ] + [pltpu.VMEM((SEC * 24, LANES), F32)] * len(sites)
-        + ([pltpu.VMEM((6, 256, 256), BF16), pltpu.VMEM((WD * 8, 2 * LANES), BF16), pltpu.VMEM((2 * WD * 8, LANES), F32)]
+        ] + [pltpu.VMEM((ROOM * 24, LANES), F32)] * len(sites)
+        + ([pltpu.VMEM((6, 256, 256), BF16), pltpu.VMEM((WD * 8, 2 * LANES), BF16), pltpu.VMEM((2 * WPAD * 8, LANES), F32)]
            if steps[0] == "L" else [pltpu.VMEM((WPAD * BLK, 4 * LANES), BF16)]),
         compiler_params=pltpu.CompilerParams(vmem_limit_bytes=16 * 1024 * 1024),
         cost_estimate=pl.CostEstimate(flops=(2000000000 if steps[0] == "L" else 50000000) * groups[1] * len(sites), bytes_accessed=100000, transcendentals=0),
@@ -290,7 +291,8 @@
 
 
 def left_operator(op):
-    return jnp.pad(op.transpose(1, 2, 3, 0), ((0, 0), (0, 0), (0, 0), (0, WPAD - WD))).reshape(WD * PHYS, LANES).astype(F32)
+    extra = (0, WPAD - WD)
+    return jnp.pad(op.transpose(1, 2, 3, 0), (extra, (0, 0), (0, 0), extra)).reshape(WPAD * PHYS, LANES).astype(F32)
 
 
 def right_operator(op):
@@ -320,7 +322,7 @@
 
 
 def to_wire(raw):
-    return call(wire_kernel, "to_wire", [(16, 160, LANES)], [raw], [pltpu.VMEM((SEC * TILES, LANES), F32)])[0]
+    return call(wire_kernel, "to_wire", [(16, 160, LANES)], [raw], [pltpu.VMEM((ROOM * TILES, LANES), F32)])[0]
 
 
 def permute_wire(order, wire, out, held):
@@ -343,7 +345,7 @@
 
 
 def permute_pack(order, chosen, wire, sites):
-    scratch = [pltpu.VMEM((16 * 160, LANES), F32), pltpu.VMEM((SEC * 24, LANES), F32)]
+    scratch = [pltpu.VMEM((16 * 160, LANES), F32), pltpu.VMEM((ROOM * 24, LANES), F32)]
     return call(permute_pack_kernel, "permute_pack", [(16, 208, LANES)], [order, chosen, wire, sites], scratch, 2)[0]
 
 
@@ -382,7 +384,7 @@
 
 
 def join(*parts):
-    return call(join_kernel, "join", [(SEC, ENV)], parts, [pltpu.VMEM((SEC * TILES, LANES), F32)])[0]
+    return call(join_kernel, "join", [(SEC, ENV)], parts, [pltpu.VMEM((ROOM * TILES, LANES), F32)])[0]
 
 
 def shifted(x, by):

time: 107 us -> 109 us (1.019); the launches traced: 105 us -> 108 us
  waiting for transfers between devices: 33.1 us -> 35.7 us
  local copies, waits for them, and re-layouts: 5.44 us -> 6.91 us
    ppermute x4, waiting for transfers between devices: 19.4 us -> 21.2 us  [shifted(): lax.ppermute(x, 'blk', [(i, (i + by) % length) for i in range(length)])]
    ppermute x4, starting transfers between devices: 10.6 us -> 8.87 us  [shifted(): lax.ppermute(x, 'blk', [(i, (i + by) % length) for i in range(length)])]
    unnamed x24, local copies, waits for them, and re-layouts: 3.16 us -> 4.46 us
    all_to_all x4, starting transfers between devices: 22.6 us -> 23.8 us  [exchanged(): return lax.all_to_all(x, 'panel', split_axis=0, concat_axis=0, tiled=True)]
  transfers between devices with their start and end apart: 8 -> 8, of which waited for: 4 -> 4; matrix products, arithmetic and copies ran while one was open for 4% -> 4% of each run, Pallas kernels for 26% -> 25%
where the time goes in v4:
time: 109 us; the launch traced here: 108 us
  waiting for transfers between devices  35.7 us (33%)
  starting transfers between devices  32.6 us (30%)
  Pallas kernels  30.3 us (28%)
  local copies, waits for them, and re-layouts  6.91 us (6%)
  other arithmetic  1.87 us (2%)
    all_to_all x4, starting transfers between devices, exchanged(): return lax.all_to_all(x, 'panel', split_axis=0, concat_axis=0, tiled=True)  23.8 us
    pallas_call x4, Pallas kernels, update(): pl.pallas_call(functools.partial(update_kernel, steps, source, result, gr...  21.5 us
    ppermute x4, waiting for transfers between devices, shifted(): lax.ppermute(x, 'blk', [(i, (i + by) % length) for i in range(length)])  21.2 us
    all_to_all x4, waiting for transfers between devices, exchanged(): return lax.all_to_all(x, 'panel', split_axis=0, concat_axis=0, tiled=True)  14.5 us
    ppermute x4, starting transfers between devices, shifted(): lax.ppermute(x, 'blk', [(i, (i + by) % length) for i in range(length)])  8.87 us
    pallas_call x6, Pallas kernels, call(): pl.pallas_call(kernel, out_shape=[jax.ShapeDtypeStruct(shape, BF16) for s...  7.61 us
    unnamed x24, local copies, waits for them, and re-layouts  4.46 us
  transfers between devices with their start and end apart: 8, of which 4 were waited for; matrix products, arithmetic and copies ran while one was open for 4% of the time, Pallas kernels for 25%

profile of v4, /device:TPU:32, one launch (start us, length us, event | category | flops | bytes accessed | tf_op | source)
XLA Modules:
  0.0 108.3 jit_solution(8082936955458127396)
XLA Ops:
  0.6 1.1 %copy-done.1 = bf16[1,20,16128]{2,1,0:T(8,128)(2,1)S(1)} copy-done((bf16[1,20,16128]{2,1,0:T(8,128)(2,1)S(1)}, bf16[1,20,16128]{2,1,0:T(8,128)(2,1)}, u32[]{:S(2)}) %copy-start.1) | copy-done | bytes 645144
  1.8 1.4 %to_wire.1 = bf16[16,160,128]{2,1,0:T(8,128)(2,1)} custom-call(bf16[20,16128]{1,0:T(8,128)(2,1)S(1)} %bitcast.26), custom_call_target="tpu_custom_call" | custom-call | flops 2000000000 | bytes 100000 | tf_op jit(solution)/shard_map/to_wire/pallas_call | solution.py:306
  3.1 7.2 %all-to-all-start = ((bf16[16,160,128]{2,1,0:T(8,128)(2,1)}), bf16[16,160,128]{2,1,0:T(8,128)(2,1)S(1)}, u32[]{:S(2)}, u32[]{:S(2)}) async-start(bf16[16,160,128]{2,1,0:T(8,128)(2,1)} %to_wire.1), calls=%async_computation | async-start | bytes 1310720 | tf_op jit(solution)/shard_map/all_to_all | solution.py:396
  10.4 0.6 copy-done.9
  11.0 0.6 copy-done.10
  12.2 2.0 %collective-permute-start.1 = (bf16[20,2432]{1,0:T(8,128)(2,1)S(1)}, bf16[20,2432]{1,0:T(8,128)(2,1)S(1)}, u32[]{:S(2)}, u32[]{:S(2)}) collective-permute-start(bf16[20,2432]{1,0:T(8,128)(2,1)S(1)} %and_select_fusion.refs_1_.sites), channel_id=1, source_target_pairs={{0,16},{16,32},{32,48},{48,64},{64,80},{80,96},{96,112},{112,128},... | collective-permute-start | bytes 291848 | tf_op jit(solution)/shard_map/ppermute | solution.py:392
  14.8 5.3 %update_l0.2 = bf16[16,160,128]{2,1,0:T(8,128)(2,1)S(1)} custom-call(bf16[20,16128]{1,0:T(8,128)(2,1)S(1)} %bitcast.27, bf16[20,2432]{1,0:T(8,128)(2,1)S(1)} %and_select_fusion.refs_1_.sites, f32[128,128]{1,0:T(8,128)S(1)} %reshape.200.refs_2_, bf16[20,128]{1,0:T(8,128)(2,1)S(1)} %slice.24.refs_3_), custom_call_target="tpu_custom_call" | custom-call | flops 8000000000 | bytes 100000 | tf_op jit(solution)/shard_map/update_l0/pallas_call | solution.py:273
  20.2 4.6 %collective-permute-start = (bf16[16,160,128]{2,1,0:T(8,128)(2,1)S(1)}, bf16[16,160,128]{2,1,0:T(8,128)(2,1)S(1)}, u32[]{:S(2)}, u32[]{:S(2)}) collective-permute-start(bf16[16,160,128]{2,1,0:T(8,128)(2,1)S(1)} %update_l0.2), channel_id=1, source_target_pairs={{0,32},{16,48},{32,64},{48,80},{64,96},{80,112},{96,128},{112,144}... | collective-permute-start | bytes 1966088 | tf_op jit(solution)/shard_map/ppermute | solution.py:392
  25.8 1.9 %permute_pack.2 = bf16[16,208,128]{2,1,0:T(8,128)(2,1)} custom-call(s32[320]{0:T(512)S(1)} %fusion.11.order, s32[32]{0:T(128)S(1)} %get-tuple-element.23.chosen, bf16[16,160,128]{2,1,0:T(8,128)(2,1)S(1)} %all-to-all-done.wire, bf16[20,2432]{1,0:T(8,128)(2,1)S(1)} %and_select_fusion.refs_1_.sites), custom_call_target="tpu_custom_call" | custom-call | flops 2000000000 | bytes 100000 | tf_op jit(solution)/shard_map/permute_pack/pallas_call | solution.py:306
  27.6 7.2 %all-to-all-start.1 = ((bf16[16,208,128]{2,1,0:T(8,128)(2,1)}), bf16[16,208,128]{2,1,0:T(8,128)(2,1)S(1)}, u32[]{:S(2)}, u32[]{:S(2)}) async-start(bf16[16,208,128]{2,1,0:T(8,128)(2,1)} %permute_pack.2), calls=%async_computation.1 | async-start | bytes 1703936 | tf_op jit(solution)/shard_map/all_to_all | solution.py:396
  35.2 0.4 multiply_bitcast_fusion
  35.6 0.3 reshape.199
  36.0 20.7 %collective-permute-done.refs_0_ = bf16[16,160,128]{2,1,0:T(8,128)(2,1)S(1)} collective-permute-done((bf16[16,160,128]{2,1,0:T(8,128)(2,1)S(1)}, bf16[16,160,128]{2,1,0:T(8,128)(2,1)S(1)}, u32[]{:S(2)}, u32[]{:S(2)}) %collective-permute-start) | collective-permute-done | bytes 655392 | tf_op jit(solution)/shard_map/ppermute | solution.py:392
  56.7 0.8 copy-done.6
  57.5 0.6 touch.2.refs_4_
  58.1 0.6 fetch.2.refs_1_
  58.7 5.8 %all-to-all-start.2 = ((bf16[16,160,128]{2,1,0:T(8,128)(2,1)}), bf16[16,160,128]{2,1,0:T(8,128)(2,1)S(1)}, u32[]{:S(2)}, u32[]{:S(2)}) async-start(bf16[16,160,128]{2,1,0:T(8,128)(2,1)} %copy-done.6), calls=%async_computation.2 | async-start | bytes 1310720 | tf_op jit(solution)/shard_map/all_to_all | solution.py:396
  64.5 5.0 %update_rr0.1 = bf16[10,128,128]{2,1,0:T(8,128)(2,1)S(1)} custom-call(bf16[16,208,128]{2,1,0:T(8,128)(2,1)S(1)} %all-to-all-done.1.wire.refs_0_, bf16[480,128]{1,0:T(8,128)(2,1)S(1)} %fetch.2.refs_1_, bf16[20,2432]{1,0:T(8,128)(2,1)S(1)} %collective-permute-done.1.refs_2_.sites, bf16[256,224]{1,0:T(8,128)(2,1)S(1)} %copy.24.refs_3_, bf16[16,128]{1,0:T(8,128)(2,1)S(1)} %copy-done), custom_call_target="tpu_custom_call" | custom-call | flops 200000000 | bytes 100000 | tf_op jit(solution)/shard_map/update_rr0/pallas_call | solution.py:273
  69.5 1.0 collective-permute-start.2
  70.6 0.8 slice_bitcast_fusion
  72.0 6.3 %all-to-all-done.2.wire = bf16[16,160,128]{2,1,0:T(8,128)(2,1)S(1)} async-done(((bf16[16,160,128]{2,1,0:T(8,128)(2,1)}), bf16[16,160,128]{2,1,0:T(8,128)(2,1)S(1)}, u32[]{:S(2)}, u32[]{:S(2)}) %all-to-all-start.2) | async-done | bytes 655392 | tf_op jit(solution)/shard_map/all_to_all | solution.py:396
  78.3 1.9 %permute_pack.3 = bf16[16,208,128]{2,1,0:T(8,128)(2,1)} custom-call(s32[320]{0:T(512)S(1)} %fusion.14.order, s32[32]{0:T(128)S(1)} %get-tuple-element.22.chosen, bf16[16,160,128]{2,1,0:T(8,128)(2,1)S(1)} %all-to-all-done.2.wire, bf16[20,2432]{1,0:T(8,128)(2,1)S(1)} %collective-permute-done.1.refs_2_.sites), custom_call_target="tpu_custom_call" | custom-call | flops 2000000000 | bytes 100000 | tf_op jit(solution)/shard_map/permute_pack/pallas_call | solution.py:306
  80.1 3.6 %all-to-all-start.3 = ((bf16[16,208,128]{2,1,0:T(8,128)(2,1)}), bf16[16,208,128]{2,1,0:T(8,128)(2,1)S(1)}, u32[]{:S(2)}, u32[]{:S(2)}) async-start(bf16[16,208,128]{2,1,0:T(8,128)(2,1)} %permute_pack.3), calls=%async_computation.3 | async-start | bytes 1703936 | tf_op jit(solution)/shard_map/all_to_all | solution.py:396
  83.7 5.0 %update_rr2.1 = bf16[10,128,128]{2,1,0:T(8,128)(2,1)S(1)} custom-call(bf16[16,208,128]{2,1,0:T(8,128)(2,1)S(1)} %all-to-all-done.1.wire.refs_0_, bf16[480,128]{1,0:T(8,128)(2,1)S(1)} %fetch.2.refs_1_, bf16[20,2432]{1,0:T(8,128)(2,1)S(1)} %collective-permute-done.1.refs_2_.sites, bf16[256,224]{1,0:T(8,128)(2,1)S(1)} %copy.24.refs_3_), custom_call_target="tpu_custom_call" | custom-call | flops 200000000 | bytes 100000 | tf_op jit(solution)/shard_map/update_rr2/pallas_call | solution.py:273
  88.8 1.3 %collective-permute-start.3 = (bf16[10,128,128]{2,1,0:T(8,128)(2,1)S(1)}, bf16[10,128,128]{2,1,0:T(8,128)(2,1)S(1)}, u32[]{:S(2)}, u32[]{:S(2)}) collective-permute-start(bf16[10,128,128]{2,1,0:T(8,128)(2,1)S(1)} %update_rr2.1), channel_id=1, source_target_pairs={{0,224},{16,240},{32,0},{48,16},{64,32},{80,48},{96,64},{112,80},{... | collective-permute-start | bytes 983048 | tf_op jit(solution)/shard_map/ppermute | solution.py:392
  90.0 0.7 copy-done.3
  90.8 0.6 touch.3.refs_3_
  91.4 8.2 %all-to-all-done.3.wire.refs_0_ = bf16[16,208,128]{2,1,0:T(8,128)(2,1)S(1)} async-done(((bf16[16,208,128]{2,1,0:T(8,128)(2,1)}), bf16[16,208,128]{2,1,0:T(8,128)(2,1)S(1)}, u32[]{:S(2)}, u32[]{:S(2)}) %all-to-all-start.3) | async-done | bytes 852000 | tf_op jit(solution)/shard_map/all_to_all | solution.py:396
  99.6 0.6 fetch.3.refs_1_
  100.3 6.1 %update_l0.3 = bf16[20,16128]{1,0:T(8,128)(2,1)} custom-call(bf16[16,208,128]{2,1,0:T(8,128)(2,1)S(1)} %all-to-all-done.3.wire.refs_0_, bf16[480,128]{1,0:T(8,128)(2,1)S(1)} %fetch.3.refs_1_, f32[128,128]{1,0:T(8,128)S(1)} %reshape.200.refs_2_, bf16[16,128]{1,0:T(8,128)(2,1)S(1)} %copy-done.5), custom_call_target="tpu_custom_call" | custom-call | flops 8000000000 | bytes 100000 | tf_op jit(solution)/shard_map/update_l0/pallas_call | solution.py:273
  106.4 0.5 collective-permute-done.3.refs_1_
  106.9 1.4 %join.1 = bf16[20,16128]{1,0:T(8,128)(2,1)} custom-call(bf16[10,128,128]{2,1,0:T(8,128)(2,1)S(1)} %copy-done.4, bf16[10,128,128]{2,1,0:T(8,128)(2,1)S(1)} %collective-permute-done.3.refs_1_), custom_call_target="tpu_custom_call" | custom-call | flops 2000000000 | bytes 100000 | tf_op jit(solution)/shard_map/join/pallas_call | solution.py:306
  (66 shorter events, 3.3 us)
Async XLA Ops:
  0.6 1.1 %copy-start.1 = (bf16[1,20,16128]{2,1,0:T(8,128)(2,1)S(1)}, bf16[1,20,16128]{2,1,0:T(8,128)(2,1)}, u32[]{:S(2)}) copy-start(bf16[1,20,16128]{2,1,0:T(8,128)(2,1)} %param.7) | copy-start | bytes 1935364
  3.1 8.8 %copy-start.8 = (bf16[1,20,2304]{2,1,0:T(8,128)(2,1)S(1)}, bf16[1,20,2304]{2,1,0:T(8,128)(2,1)}, u32[]{:S(2)}) copy-start(bf16[1,20,2304]{2,1,0:T(8,128)(2,1)} %param.8) | copy-start | bytes 276484
  3.1 22.7 %all-to-all-start = ((bf16[16,160,128]{2,1,0:T(8,128)(2,1)}), bf16[16,160,128]{2,1,0:T(8,128)(2,1)S(1)}, u32[]{:S(2)}, u32[]{:S(2)}) async-start(bf16[16,160,128]{2,1,0:T(8,128)(2,1)} %to_wire.1), calls=%async_computation | async-start | bytes 1310720 | tf_op jit(solution)/shard_map/all_to_all | solution.py:396
  10.4 0.7 copy-start.9
  11.0 0.7 copy-start.10
  12.0 2.2 %copy-start.7 = (bf16[28,28,4,4]{1,3,2,0:T(4,128)(2,1)S(1)}, bf16[28,28,4,4]{1,3,2,0:T(4,128)(2,1)}, u32[]{:S(2)}) copy-start(bf16[28,28,4,4]{1,3,2,0:T(4,128)(2,1)} %param.9) | copy-start | bytes 75268
  12.2 2.7 %copy-start.2 = (bf16[1,20,16128]{2,1,0:T(8,128)(2,1)S(1)}, bf16[1,20,16128]{2,1,0:T(8,128)(2,1)}, u32[]{:S(2)}) copy-start(bf16[1,20,16128]{2,1,0:T(8,128)(2,1)} %param.6) | copy-start | bytes 1935364
  12.2 12.6 %collective-permute-start.1 = (bf16[20,2432]{1,0:T(8,128)(2,1)S(1)}, bf16[20,2432]{1,0:T(8,128)(2,1)S(1)}, u32[]{:S(2)}, u32[]{:S(2)}) collective-permute-start(bf16[20,2432]{1,0:T(8,128)(2,1)S(1)} %and_select_fusion.refs_1_.sites), channel_id=1, source_target_pairs={{0,16},{16,32},{32,48},{48,64},{64,80},{80,96},{96,112},{112,128},... | collective-permute-start | bytes 291848 | tf_op jit(solution)/shard_map/ppermute | solution.py:392
  20.2 36.5 %collective-permute-start = (bf16[16,160,128]{2,1,0:T(8,128)(2,1)S(1)}, bf16[16,160,128]{2,1,0:T(8,128)(2,1)S(1)}, u32[]{:S(2)}, u32[]{:S(2)}) collective-permute-start(bf16[16,160,128]{2,1,0:T(8,128)(2,1)S(1)} %update_l0.2), channel_id=1, source_target_pairs={{0,32},{16,48},{32,64},{48,80},{64,96},{80,112},{96,128},{112,144}... | collective-permute-start | bytes 1966088 | tf_op jit(solution)/shard_map/ppermute | solution.py:392
  27.6 30.5 %all-to-all-start.1 = ((bf16[16,208,128]{2,1,0:T(8,128)(2,1)}), bf16[16,208,128]{2,1,0:T(8,128)(2,1)S(1)}, u32[]{:S(2)}, u32[]{:S(2)}) async-start(bf16[16,208,128]{2,1,0:T(8,128)(2,1)} %permute_pack.2), calls=%async_computation.1 | async-start | bytes 1703936 | tf_op jit(solution)/shard_map/all_to_all | solution.py:396
  56.7 0.8 copy-start.6
  58.7 5.8 %copy-start = (bf16[16,128]{1,0:T(8,128)(2,1)S(1)}, bf16[16,128]{1,0:T(8,128)(2,1)}, u32[]{:S(2)}) copy-start(bf16[16,128]{1,0:T(8,128)(2,1)} %touch.2.refs_4_) | copy-start | bytes 12292
  58.7 19.5 %all-to-all-start.2 = ((bf16[16,160,128]{2,1,0:T(8,128)(2,1)}), bf16[16,160,128]{2,1,0:T(8,128)(2,1)S(1)}, u32[]{:S(2)}, u32[]{:S(2)}) async-start(bf16[16,160,128]{2,1,0:T(8,128)(2,1)} %copy-done.6), calls=%async_computation.2 | async-start | bytes 1310720 | tf_op jit(solution)/shard_map/all_to_all | solution.py:396
  69.5 20.5 %collective-permute-start.2 = (bf16[10,128,128]{2,1,0:T(8,128)(2,1)S(1)}, bf16[10,128,128]{2,1,0:T(8,128)(2,1)S(1)}, u32[]{:S(2)}, u32[]{:S(2)}) collective-permute-start(bf16[10,128,128]{2,1,0:T(8,128)(2,1)S(1)} %update_rr0.1), channel_id=1, source_target_pairs={{0,224},{16,240},{32,0},{48,16},{64,32},{80,48},{96,64},{112,80},{... | collective-permute-start | bytes 983048 | tf_op jit(solution)/shard_map/ppermute | solution.py:392
  80.1 19.5 %all-to-all-start.3 = ((bf16[16,208,128]{2,1,0:T(8,128)(2,1)}), bf16[16,208,128]{2,1,0:T(8,128)(2,1)S(1)}, u32[]{:S(2)}, u32[]{:S(2)}) async-start(bf16[16,208,128]{2,1,0:T(8,128)(2,1)} %permute_pack.3), calls=%async_computation.3 | async-start | bytes 1703936 | tf_op jit(solution)/shard_map/all_to_all | solution.py:396
  88.8 18.2 %collective-permute-start.3 = (bf16[10,128,128]{2,1,0:T(8,128)(2,1)S(1)}, bf16[10,128,128]{2,1,0:T(8,128)(2,1)S(1)}, u32[]{:S(2)}, u32[]{:S(2)}) collective-permute-start(bf16[10,128,128]{2,1,0:T(8,128)(2,1)S(1)} %update_rr2.1), channel_id=1, source_target_pairs={{0,224},{16,240},{32,0},{48,16},{64,32},{80,48},{96,64},{112,80},{... | collective-permute-start | bytes 983048 | tf_op jit(solution)/shard_map/ppermute | solution.py:392
  90.0 0.7 copy-start.3
  99.6 0.7 copy-start.5
  100.3 6.7 %copy-start.4 = (bf16[10,128,128]{2,1,0:T(8,128)(2,1)S(1)}, bf16[10,128,128]{2,1,0:T(8,128)(2,1)}, u32[]{:S(2)}) copy-start(bf16[10,128,128]{2,1,0:T(8,128)(2,1)} %copy-done.3) | copy-start | bytes 983044
